TPU v7x, 512 devices: a whole 4x4x16 slice. The times are simulated.
512 devices in a mesh: member: 8 (over y_hi, x), space: 64 (over z, y_lo, core).
Axes of the slice: x: 4, y: 4 (y_hi: 2, y_lo: 2; y = y_hi * 2 + y_lo), z: 16, core: 2. Of those that a mesh axis runs over, the one named last changes fastest.
Arguments:
- latent: bfloat16 [8, 4096, 1024], P('member', 'space'), may hold values from -6 to 6
- neighbours: int32 [4, 32768], P(None, 'space'), may hold values from 0 to 4095, as said below
- live: int32 [4, 32768], P(None, 'space'), may hold values 0 or 1
- edge_weight: bfloat16 [4, 32768], P(None, 'space'), may hold values from 0.19921875 to 1
- area: float32 [32768], P('space'), may hold values from 0.5 to 4
- targets: float32 [100, 32768], P(None, 'space'), may hold values from -5 to 5
- w_in: bfloat16 [1024, 1024], replicated, may hold values from -0.1875 to 0.1875
- w_out: bfloat16 [100, 1024], replicated, may hold values from -0.1875 to 0.1875
Outputs:
- grad_latent: bfloat16 [8, 4096, 1024], P('member', 'space')
Inputs may be any that keep to these rules, and one draw needn't show every extreme that they name: `neighbours`: grid point g = s * 512 + j (space shard s) names in each slot a mesh node within 32 places, cyclically modulo 4096, of node s * 64 + floor(j * 64 / 512); the 4 slots of one grid point name distinct nodes; the first and last grid point of every shard reach the full distance 32 below and above.
All inputs are finite; a program needn't handle non-finite values. No bound on the sum of `live` on one device may be relied on, other than what follows from the above.
Results may differ from a plain program's by a relative error of at most 0.01.
Values may be sent and summed in bfloat16 or wider, within the bound.
No kernel may reach another device: no remote copies, remote signals or barrier semaphores. Data moves between devices by JAX's collectives and lax.ppermute only.
A program may use at most 64 MiB of HBM per device.

v0:
```python
import jax
import jax.numpy as jnp
from jax import lax
from jax.sharding import PartitionSpec as P

HALO = 32


smooth = 0.0025


def extended_2(block, sides, width):
    for axis, dim in sides:
        count = lax.axis_size(axis)
        forward = [(i, i + 1) for i in range(count - 1)]
        forward.append((count - 1, 0))
        backward = [(target, source) for source, target in forward]
        low = lax.ppermute(
            lax.slice_in_dim(block, block.shape[dim] - width, None, axis=dim), axis, forward
        )
        high = lax.ppermute(lax.slice_in_dim(block, 0, width, axis=dim), axis, backward)
        block = jnp.concatenate([low, block, high], axis=dim)
    return block


def from_behind(shard, axis, by):
    size = lax.axis_size(axis)
    return lax.ppermute(shard, axis, [(i, (i + by) % size) for i in range(size)])


def slope(diff):
    return diff / jnp.sqrt(diff * diff + smooth)


def per_device(latent, neighbours, live, edge_weight, area, targets, w_in, w_out):
    rows = latent.shape[1]
    spaces = lax.axis_size("space")
    members = lax.axis_size("member") * latent.shape[0]
    offset = lax.axis_index("space") * rows - HALO
    extended = extended_2(latent[0], (("space", 0),), HALO)
    span_rows = rows + 2 * HALO
    local_rows = jnp.mod(neighbours - offset, rows * spaces)
    coef = edge_weight * live.astype(jnp.bfloat16)
    column = jnp.arange(span_rows, dtype=jnp.int32)
    picks = jnp.where(
        local_rows[:, :, None] == column[None, None, :],
        coef[:, :, None],
        jnp.zeros((), jnp.bfloat16),
    )
    adjacency = jnp.sum(picks, axis=0, dtype=jnp.bfloat16)
    joined = jnp.dot(adjacency, extended, preferred_element_type=jnp.float32).astype(jnp.bfloat16)
    pre = jnp.dot(joined, w_in, preferred_element_type=jnp.float32)
    hidden = jax.nn.silu(pre).astype(jnp.bfloat16)
    field = lax.dot_general(
        w_out, hidden, (((1,), (1,)), ((), ())), preferred_element_type=jnp.float32
    )
    own_term = slope(field - targets)
    every = lax.all_gather(field[None], "member", axis=0, tiled=True)
    pairwise = jnp.sum(slope(field[None] - every), axis=0)
    grad_field = (area[None, :] * (own_term - pairwise / (members - 1))).astype(jnp.bfloat16)
    grad_hidden = lax.dot_general(
        grad_field, w_out, (((0,), (0,)), ((), ())), preferred_element_type=jnp.float32
    )
    sigma = jax.nn.sigmoid(pre)
    grad_pre = (grad_hidden * sigma * (1.0 + pre * (1.0 - sigma))).astype(jnp.bfloat16)
    grad_joined = lax.dot_general(
        grad_pre, w_in, (((1,), (1,)), ((), ())), preferred_element_type=jnp.float32
    ).astype(jnp.bfloat16)
    grad_extended = lax.dot_general(
        adjacency, grad_joined, (((0,), (0,)), ((), ())), preferred_element_type=jnp.float32
    )
    upper_rim = grad_extended[:HALO]
    lower_rim = grad_extended[span_rows - HALO :]
    from_after = from_behind(upper_rim, "space", -1)
    from_before = from_behind(lower_rim, "space", 1)
    inner = grad_extended[HALO : HALO + rows]
    inner = inner.at[:HALO].add(from_before)
    inner = inner.at[rows - HALO :].add(from_after)
    return inner.astype(jnp.bfloat16)[None]


def solution(mesh):
    return jax.shard_map(
        per_device,
        mesh=mesh,
        in_specs=(
            P("member", "space", None),
            P(None, "space"),
            P(None, "space"),
            P(None, "space"),
            P("space"),
            P(None, "space"),
            P(),
            P(),
        ),
        out_specs=P("member", "space", None),
        check_vma=False,
    )
```

profile of v0, /device:TPU:1, one launch (start us, length us, event | category | flops | bytes accessed | tf_op | source)
XLA Modules:
  0.0 122.8 jit_solution(7908405406428866163)
XLA Ops:
  6.5 0.0 copy-start
  6.5 0.0 all-gather.4.cloned.1.call-start
  6.5 1.0 slice_bitcast_fusion.1
  7.6 4.6 %collective-permute-start = (bf16[32,1024]{1,0:T(8,128)(2,1)S(1)}, bf16[32,1024]{1,0:T(8,128)(2,1)S(1)}, u32[]{:S(2)}, u32[]{:S(2)}) collective-permute-start(bf16[32,1024]{1,0:T(8,128)(2,1)S(1)} %get-tuple-element.31), channel_id=1, source_target_pairs={{0,1},{1,2},{2,3},{3,4},{4,5},{5,6},{6,7},{7,8},{8,9},{9,10},{10,1... | collective-permute-start | bytes 196616 | tf_op jit(solution)/shard_map/ppermute | solution.py:18
  12.2 6.1 %collective-permute-start.1 = (bf16[32,1024]{1,0:T(8,128)(2,1)S(1)}, bf16[32,1024]{1,0:T(8,128)(2,1)S(1)}, u32[]{:S(2)}, u32[]{:S(2)}) collective-permute-start(bf16[32,1024]{1,0:T(8,128)(2,1)S(1)} %get-tuple-element.32), channel_id=1, source_target_pairs={{1,0},{2,1},{3,2},{4,3},{5,4},{6,5},{7,6},{8,7},{9,8},{10,9},{11,1... | collective-permute-start | bytes 196616 | tf_op jit(solution)/shard_map/ppermute | solution.py:21
  18.3 0.7 convert_multiply_fusion
  19.0 0.7 add_select_fusion
  19.7 0.7 fusion.4
  20.5 0.0 collective-permute-done
  20.5 0.0 collective-permute-done.1
  20.5 0.0 copy-done
  20.5 0.0 copy-start.2
  20.5 3.8 %fusion = f32[512,1024]{1,0:T(8,128)} fusion(bf16[1024,1024]{1,0:T(8,128)(2,1)S(1)} %copy-done, bf16[512,128]{1,0:T(8,128)(2,1)S(1)} %fusion.4, bf16[32,1024]{1,0:T(8,128)(2,1)S(1)} %collective-permute-done.1, bf16[64,1024]{1,0:T(8,128)(2,1)} %bitcast.23, bf16[32,1024]{1,0:T(8,128)(2,1)S(1)} %collective-permute-done), kind=kOutput, calls=%fused_computation.6 | convolution fusion | flops 1209270272 | bytes 4587520 | tf_op jit(solution)/shard_map/dot_general | solution.py:52
  24.3 0.0 copy-done.2
  24.3 3.0 %fusion.3 = f32[512,100]{0,1:T(8,128)} fusion(bf16[100,1024]{1,0:T(8,128)(2,1)S(1)} %copy-done.2, f32[512,1024]{1,0:T(8,128)} %fusion), kind=kOutput, calls=%fused_computation.10 | convolution fusion | flops 107479040 | bytes 2506752 | tf_op jit(solution)/shard_map/dot_general | solution.py:54
  27.3 0.0 copy-start.1
  27.3 0.0 copy-start.3
  27.3 0.0 copy-start.4
  27.3 0.0 all-gather.4.cloned.1.call-update
  27.3 68.4 %all-gather.4.cloned.1.call-done = f32[8,100,512]{2,1,0:T(8,128)} async-done(((f32[1,100,512]{2,1,0:T(8,128)}), f32[8,100,512]{2,1,0:T(8,128)}) %all-gather.4.cloned.1.call-update) | async-done | bytes 1638416 | tf_op jit(solution)/shard_map/all_gather | solution.py:58
  95.8 1.8 %multiply_reduce_fusion = f32[100,512]{1,0:T(8,128)S(1)} fusion(f32[8,100,512]{2,1,0:T(8,128)} %all-gather.4.cloned.1.call-done, f32[100,512]{1,0:T(8,128)} %bitcast.22), kind=kLoop, calls=%fused_computation.3 | loop fusion | flops 1996800 | bytes 2048000 | tf_op jit(solution)/shard_map/reduce_sum | solution.py:59
  97.6 0.0 copy-done.1
  97.6 0.0 copy-done.3
  97.6 0.0 copy-done.4
  97.6 3.5 %multiply_convert_fusion = bf16[512,1024]{1,0:T(8,128)(2,1)} fusion(f32[512,1024]{1,0:T(8,128)} %fusion, bf16[100,1024]{1,0:T(8,128)(2,1)S(1)} %copy-done.2, f32[100,512]{1,0:T(8,128)S(1)} %multiply_reduce_fusion, f32[100,512]{1,0:T(8,128)S(1)} %copy-done.3, f32[512]{0:T(512)S(1)} %copy-done.4, f32[512,100]{0,1:T(8,128)S(1)} %copy-done.1), kind=kOutput, calls=%fused_computation | convolution fusion | flops 109985792 | bytes 3966976 | tf_op jit(solution)/shard_map/dot_general | solution.py:61
  101.1 2.7 %fusion.1 = f32[128,1024]{1,0:T(8,128)S(1)} fusion(bf16[512,128]{1,0:T(8,128)(2,1)S(1)} %fusion.4, bf16[512,1024]{1,0:T(8,128)(2,1)} %multiply_convert_fusion, bf16[1024,1024]{1,0:T(8,128)(2,1)S(1)} %copy-done), kind=kOutput, calls=%fused_computation.7 | convolution fusion | flops 1208483840 | bytes 3801088 | tf_op jit(solution)/shard_map/dot_general | solution.py:69
  103.8 4.4 %collective-permute-start.2 = (f32[32,1024]{1,0:T(8,128)S(1)}, f32[32,1024]{1,0:T(8,128)S(1)}, u32[]{:S(2)}, u32[]{:S(2)}) collective-permute-start(f32[32,1024]{1,0:T(8,128)S(1)} %get-tuple-element.30), channel_id=1, source_target_pairs={{0,1},{1,2},{2,3},{3,4},{4,5},{5,6},{6,7},{7,8},{8,9},{9,10},{10,1... | collective-permute-start | bytes 393224 | tf_op jit(solution)/shard_map/ppermute | solution.py:28
  108.2 1.9 %collective-permute-start.3 = (f32[32,1024]{1,0:T(8,128)S(1)}, f32[32,1024]{1,0:T(8,128)S(1)}, u32[]{:S(2)}, u32[]{:S(2)}) collective-permute-start(f32[32,1024]{1,0:T(8,128)S(1)} %get-tuple-element.29), channel_id=1, source_target_pairs={{0,63},{1,0},{2,1},{3,2},{4,3},{5,4},{6,5},{7,6},{8,7},{9,8},{10,9... | collective-permute-start | bytes 393224 | tf_op jit(solution)/shard_map/ppermute | solution.py:28
  110.2 0.0 collective-permute-done.2
  110.2 5.0 %collective-permute-done.3 = f32[32,1024]{1,0:T(8,128)S(1)} collective-permute-done((f32[32,1024]{1,0:T(8,128)S(1)}, f32[32,1024]{1,0:T(8,128)S(1)}, u32[]{:S(2)}, u32[]{:S(2)}) %collective-permute-start.3) | collective-permute-done | bytes 131104 | tf_op jit(solution)/shard_map/ppermute | solution.py:28
  115.2 0.7 convert_bitcast_fusion
  (4 shorter events, 0.1 us)
Async XLA Ops:
  6.5 14.0 %copy-start = (bf16[1024,1024]{1,0:T(8,128)(2,1)S(1)}, bf16[1024,1024]{1,0:T(8,128)(2,1)}, u32[]{:S(2)}) copy-start(bf16[1024,1024]{1,0:T(8,128)(2,1)} %param.18) | copy-start | bytes 6291460
  6.5 89.2 %all-gather.4.cloned.1.call-start = ((), (), s32[]{:S(2)}) async-start(), calls=%async_computation | async-start | bytes 1916928 | tf_op jit(solution)/shard_map/all_gather | solution.py:58
  7.6 12.9 %collective-permute-start = (bf16[32,1024]{1,0:T(8,128)(2,1)S(1)}, bf16[32,1024]{1,0:T(8,128)(2,1)S(1)}, u32[]{:S(2)}, u32[]{:S(2)}) collective-permute-start(bf16[32,1024]{1,0:T(8,128)(2,1)S(1)} %get-tuple-element.31), channel_id=1, source_target_pairs={{0,1},{1,2},{2,3},{3,4},{4,5},{5,6},{6,7},{7,8},{8,9},{9,10},{10,1... | collective-permute-start | bytes 196616 | tf_op jit(solution)/shard_map/ppermute | solution.py:18
  12.2 8.3 %collective-permute-start.1 = (bf16[32,1024]{1,0:T(8,128)(2,1)S(1)}, bf16[32,1024]{1,0:T(8,128)(2,1)S(1)}, u32[]{:S(2)}, u32[]{:S(2)}) collective-permute-start(bf16[32,1024]{1,0:T(8,128)(2,1)S(1)} %get-tuple-element.32), channel_id=1, source_target_pairs={{1,0},{2,1},{3,2},{4,3},{5,4},{6,5},{7,6},{8,7},{9,8},{10,9},{11,1... | collective-permute-start | bytes 196616 | tf_op jit(solution)/shard_map/ppermute | solution.py:21
  20.5 3.8 %copy-start.2 = (bf16[100,1024]{1,0:T(8,128)(2,1)S(1)}, bf16[100,1024]{1,0:T(8,128)(2,1)}, u32[]{:S(2)}) copy-start(bf16[100,1024]{1,0:T(8,128)(2,1)} %param.19) | copy-start | bytes 614404
  27.3 70.3 %copy-start.1 = (f32[512,100]{0,1:T(8,128)S(1)}, f32[512,100]{0,1:T(8,128)}, u32[]{:S(2)}) copy-start(f32[512,100]{0,1:T(8,128)} %fusion.3) | copy-start | bytes 614404
  27.3 70.3 %copy-start.3 = (f32[100,512]{1,0:T(8,128)S(1)}, f32[100,512]{1,0:T(8,128)}, u32[]{:S(2)}) copy-start(f32[100,512]{1,0:T(8,128)} %param.17) | copy-start | bytes 614404
  27.3 70.3 %copy-start.4 = (f32[512]{0:T(512)S(1)}, f32[512]{0:T(512)}, u32[]{:S(2)}) copy-start(f32[512]{0:T(512)} %param.16) | copy-start | bytes 6148
  103.8 6.3 %collective-permute-start.2 = (f32[32,1024]{1,0:T(8,128)S(1)}, f32[32,1024]{1,0:T(8,128)S(1)}, u32[]{:S(2)}, u32[]{:S(2)}) collective-permute-start(f32[32,1024]{1,0:T(8,128)S(1)} %get-tuple-element.30), channel_id=1, source_target_pairs={{0,1},{1,2},{2,3},{3,4},{4,5},{5,6},{6,7},{7,8},{8,9},{9,10},{10,1... | collective-permute-start | bytes 393224 | tf_op jit(solution)/shard_map/ppermute | solution.py:28
  108.2 7.0 %collective-permute-start.3 = (f32[32,1024]{1,0:T(8,128)S(1)}, f32[32,1024]{1,0:T(8,128)S(1)}, u32[]{:S(2)}, u32[]{:S(2)}) collective-permute-start(f32[32,1024]{1,0:T(8,128)S(1)} %get-tuple-element.29), channel_id=1, source_target_pairs={{0,63},{1,0},{2,1},{3,2},{4,3},{5,4},{6,5},{7,6},{8,7},{9,8},{10,9... | collective-permute-start | bytes 393224 | tf_op jit(solution)/shard_map/ppermute | solution.py:28
Sparse Core Ops, SparseCore 0:
  27.5 68.2 all-gather.3
where the time goes:
time: 125 us; the launch traced here: 123 us
  waiting for transfers between devices  73.5 us (59%)
  starting transfers between devices  17 us (14%)
  between operations  13.5 us (11%)
  matrix products  13 us (10%)
  other arithmetic  4.69 us (4%)
    all_gather x1, waiting for transfers between devices, per_device(): every = lax.all_gather(field[None], 'member', axis=0, tiled=True)  68.4 us
    ppermute x2, starting transfers between devices, from_behind(): lax.ppermute(shard, axis, [(i, (i + by) % size) for i in range(size)])  6.29 us
    ppermute x1, starting transfers between devices, extended_2(): lax.ppermute(lax.slice_in_dim(block, 0, width, axis=dim), axis, backward)  6.11 us
    ppermute x2, waiting for transfers between devices, from_behind(): lax.ppermute(shard, axis, [(i, (i + by) % size) for i in range(size)])  5.02 us
    ppermute x1, starting transfers between devices, extended_2(): lax.ppermute(lax.slice_in_dim(block, block.shape[dim] - width, None, axis...  4.59 us
    dot_general x1, matrix products, per_device(): pre = jnp.dot(joined, w_in, preferred_element_type=jnp.float32)  3.8 us
    dot_general x1, matrix products, per_device(): lax.dot_general(grad_field, w_out, (((0,), (0,)), ((), ())), preferred_el...  3.51 us
    dot_general x1, matrix products, per_device(): lax.dot_general(w_out, hidden, (((1,), (1,)), ((), ())), preferred_elemen...  3.01 us
  transfers between devices with their start and end apart: 5, of which 2 were waited for; matrix products, arithmetic and copies ran while one was open for 2% of the time, Pallas kernels for 0%

commit v1 on v0

--- a/solution.py
+++ b/solution.py
@@ -55,8 +55,12 @@
         w_out, hidden, (((1,), (1,)), ((), ())), preferred_element_type=jnp.float32
     )
     own_term = slope(field - targets)
-    every = lax.all_gather(field[None], "member", axis=0, tiled=True)
-    pairwise = jnp.sum(slope(field[None] - every), axis=0)
+    copies = jnp.broadcast_to(field.astype(jnp.bfloat16)[None], (members,) + field.shape)
+    every = lax.all_to_all(copies, "member", 0, 0, tiled=True)
+    me = lax.axis_index("member")
+    others = (jnp.arange(members) != me)[:, None, None]
+    diffs = field[None] - every.astype(jnp.float32)
+    pairwise = jnp.sum(jnp.where(others, slope(diffs), 0.0), axis=0)
     grad_field = (area[None, :] * (own_term - pairwise / (members - 1))).astype(jnp.bfloat16)
     grad_hidden = lax.dot_general(
         grad_field, w_out, (((0,), (0,)), ((), ())), preferred_element_type=jnp.float32

time: 125 us -> 62.2 us (0.50)
  the two profiles are of different devices: /device:TPU:1 before, /device:TPU:2 now
where the time goes in v1:
time: 62.2 us; the launch traced here: 61.7 us
  starting transfers between devices  30.4 us (49%)
  waiting for transfers between devices  13.3 us (21%)
  matrix products  12.4 us (20%)
  other arithmetic  3.33 us (5%)
  local copies, waits for them, and re-layouts  2.04 us (3%)
    ppermute x1, starting transfers between devices, extended_2(): lax.ppermute(lax.slice_in_dim(block, 0, width, axis=dim), axis, backward)  11.9 us
    all_to_all x1, waiting for transfers between devices, per_device(): every = lax.all_to_all(copies, 'member', 0, 0, tiled=True)  10.8 us
    ppermute x2, starting transfers between devices, from_behind(): lax.ppermute(shard, axis, [(i, (i + by) % size) for i in range(size)])  9.51 us
    all_to_all x1, starting transfers between devices, per_device(): every = lax.all_to_all(copies, 'member', 0, 0, tiled=True)  7.17 us
    dot_general x1, matrix products, per_device(): pre = jnp.dot(joined, w_in, preferred_element_type=jnp.float32)  3.81 us
    dot_general x1, matrix products, per_device(): lax.dot_general(grad_field, w_out, (((0,), (0,)), ((), ())), preferred_el...  3.66 us
    dot_general x1, matrix products, per_device(): lax.dot_general(adjacency, grad_joined, (((0,), (0,)), ((), ())), preferr...  2.66 us
    ppermute x2, waiting for transfers between devices, from_behind(): lax.ppermute(shard, axis, [(i, (i + by) % size) for i in range(size)])  2.48 us
  transfers between devices with their start and end apart: 5, of which 3 were waited for; matrix products, arithmetic and copies ran while one was open for 4% of the time, Pallas kernels for 0%

profile of v1, /device:TPU:2, one launch (start us, length us, event | category | flops | bytes accessed | tf_op | source)
XLA Modules:
  0.0 61.7 jit_solution(9113681289550676165)
XLA Ops:
  0.0 0.0 copy-start
  0.0 1.0 %slice_bitcast_fusion.1 = (bf16[32,1024]{1,0:T(8,128)(2,1)S(1)}, bf16[32,1024]{1,0:T(8,128)(2,1)S(1)}) fusion(bf16[1,64,1024]{2,1,0:T(8,128)(2,1)} %param.12), kind=kLoop, calls=%fused_computation.27 | loop fusion | bytes 262144 | tf_op jit(solution)/shard_map/slice | solution.py:19
  1.0 1.9 %collective-permute-start = (bf16[32,1024]{1,0:T(8,128)(2,1)S(1)}, bf16[32,1024]{1,0:T(8,128)(2,1)S(1)}, u32[]{:S(2)}, u32[]{:S(2)}) collective-permute-start(bf16[32,1024]{1,0:T(8,128)(2,1)S(1)} %get-tuple-element.31), channel_id=1, source_target_pairs={{0,1},{1,2},{2,3},{3,4},{4,5},{5,6},{6,7},{7,8},{8,9},{9,10},{10,1... | collective-permute-start | bytes 196616 | tf_op jit(solution)/shard_map/ppermute | solution.py:18
  3.0 11.9 %collective-permute-start.1 = (bf16[32,1024]{1,0:T(8,128)(2,1)S(1)}, bf16[32,1024]{1,0:T(8,128)(2,1)S(1)}, u32[]{:S(2)}, u32[]{:S(2)}) collective-permute-start(bf16[32,1024]{1,0:T(8,128)(2,1)S(1)} %get-tuple-element.32), channel_id=1, source_target_pairs={{1,0},{2,1},{3,2},{4,3},{5,4},{6,5},{7,6},{8,7},{9,8},{10,9},{11,1... | collective-permute-start | bytes 196616 | tf_op jit(solution)/shard_map/ppermute | solution.py:21
  14.8 0.7 %convert_multiply_fusion = bf16[4,512]{1,0:T(4,128)(2,1)S(1)} fusion(bf16[4,512]{1,0:T(4,128)(2,1)} %param.15, s32[4,512]{1,0:T(4,128)} %param.14), kind=kLoop, calls=%fused_computation.32 | loop fusion | flops 4096 | bytes 16384 | tf_op jit(solution)/shard_map/mul | solution.py:43
  15.6 0.7 %add_select_fusion = s32[4,512]{1,0:T(4,128)S(1)} fusion(s32[4,512]{1,0:T(4,128)} %param.13, s32[]{:T(128)S(6)} %sub.26), kind=kLoop, calls=%fused_computation.28 | loop fusion | flops 24576 | bytes 16388 | tf_op jit(solution)/shard_map/jit(remainder)/select_n | solution.py:42
  16.3 0.7 %fusion.3 = bf16[512,128]{1,0:T(8,128)(2,1)S(1)} fusion(s32[4,512]{1,0:T(4,128)S(1)} %add_select_fusion, bf16[4,512]{1,0:T(4,128)(2,1)S(1)} %convert_multiply_fusion), kind=kLoop, calls=%fused_computation.11 | loop fusion | flops 720896 | bytes 143360 | tf_op jit(solution)/shard_map/reduce_sum | solution.py:50
  17.0 0.0 collective-permute-done
  17.0 0.0 collective-permute-done.1
  17.0 0.0 copy-done
  17.0 0.0 copy-start.1
  17.0 3.8 %fusion = f32[512,1024]{1,0:T(8,128)} fusion(bf16[1024,1024]{1,0:T(8,128)(2,1)S(1)} %copy-done, bf16[512,128]{1,0:T(8,128)(2,1)S(1)} %fusion.3, bf16[32,1024]{1,0:T(8,128)(2,1)S(1)} %collective-permute-done.1, bf16[64,1024]{1,0:T(8,128)(2,1)} %bitcast.16, bf16[32,1024]{1,0:T(8,128)(2,1)S(1)} %collective-permute-done), kind=kOutput, calls=%fused_computation.6 | convolution fusion | flops 1209270272 | bytes 4587520 | tf_op jit(solution)/shard_map/dot_general | solution.py:52
  20.8 0.0 copy-done.1
  20.8 2.3 %fusion.26 = (bf16[100,512]{1,0:T(8,128)(2,1)S(1)}, f32[100,512]{1,0:T(8,128)S(1)}) fusion(bf16[100,1024]{1,0:T(8,128)(2,1)S(1)} %copy-done.1, f32[512,1024]{1,0:T(8,128)} %fusion), kind=kOutput, calls=%fused_computation.39 | convolution fusion | flops 107530240 | bytes 2609152 | tf_op jit(solution)/shard_map/dot_general | solution.py:54
  23.2 0.0 copy-start.2
  23.2 1.0 %broadcast_in_dim.42 = bf16[8,100,512]{2,1,0:T(8,128)(2,1)} broadcast(bf16[100,512]{1,0:T(8,128)(2,1)S(1)} %get-tuple-element.33), dimensions={1,2} | broadcast | bytes 921600 | tf_op jit(solution)/shard_map/broadcast_in_dim | solution.py:58
  24.1 7.2 %all-to-all-start = ((bf16[8,100,512]{2,1,0:T(8,128)(2,1)}), bf16[8,100,512]{2,1,0:T(8,128)(2,1)S(1)}, u32[]{:S(2)}, u32[]{:S(2)}) async-start(bf16[8,100,512]{2,1,0:T(8,128)(2,1)} %broadcast_in_dim.42), calls=%async_computation | async-start | bytes 1703936 | tf_op jit(solution)/shard_map/all_to_all | solution.py:59
  31.3 10.8 %all-to-all-done = bf16[8,100,512]{2,1,0:T(8,128)(2,1)S(1)} async-done(((bf16[8,100,512]{2,1,0:T(8,128)(2,1)}), bf16[8,100,512]{2,1,0:T(8,128)(2,1)S(1)}, u32[]{:S(2)}, u32[]{:S(2)}) %all-to-all-start) | async-done | bytes 819232 | tf_op jit(solution)/shard_map/all_to_all | solution.py:59
  42.1 0.5 select_reduce_fusion
  42.6 0.0 copy-done.2
  42.6 3.7 %multiply_convert_fusion = bf16[512,1024]{1,0:T(8,128)(2,1)} fusion(f32[512,1024]{1,0:T(8,128)} %fusion, bf16[100,1024]{1,0:T(8,128)(2,1)S(1)} %copy-done.1, f32[100,512]{1,0:T(8,128)S(1)} %select_reduce_fusion, f32[100,512]{1,0:T(8,128)S(1)} %get-tuple-element.34, f32[100,512]{1,0:T(8,128)} %param.17, f32[512]{0:T(512)S(1)} %copy-done.2), kind=kOutput, calls=%fused_computation | convolution fusion | flops 109985792 | bytes 3966976 | tf_op jit(solution)/shard_map/dot_general | solution.py:65
  46.2 2.7 %fusion.1 = f32[128,1024]{1,0:T(8,128)S(1)} fusion(bf16[512,128]{1,0:T(8,128)(2,1)S(1)} %fusion.3, bf16[512,1024]{1,0:T(8,128)(2,1)} %multiply_convert_fusion, bf16[1024,1024]{1,0:T(8,128)(2,1)S(1)} %copy-done), kind=kOutput, calls=%fused_computation.7 | convolution fusion | flops 1208483840 | bytes 3801088 | tf_op jit(solution)/shard_map/dot_general | solution.py:73
  48.9 1.9 %collective-permute-start.2 = (f32[32,1024]{1,0:T(8,128)S(1)}, f32[32,1024]{1,0:T(8,128)S(1)}, u32[]{:S(2)}, u32[]{:S(2)}) collective-permute-start(f32[32,1024]{1,0:T(8,128)S(1)} %get-tuple-element.30), channel_id=1, source_target_pairs={{0,1},{1,2},{2,3},{3,4},{4,5},{5,6},{6,7},{7,8},{8,9},{9,10},{10,1... | collective-permute-start | bytes 393224 | tf_op jit(solution)/shard_map/ppermute | solution.py:28
  50.9 7.6 %collective-permute-start.3 = (f32[32,1024]{1,0:T(8,128)S(1)}, f32[32,1024]{1,0:T(8,128)S(1)}, u32[]{:S(2)}, u32[]{:S(2)}) collective-permute-start(f32[32,1024]{1,0:T(8,128)S(1)} %get-tuple-element.29), channel_id=1, source_target_pairs={{0,63},{1,0},{2,1},{3,2},{4,3},{5,4},{6,5},{7,6},{8,7},{9,8},{10,9... | collective-permute-start | bytes 393224 | tf_op jit(solution)/shard_map/ppermute | solution.py:28
  58.5 0.7 %collective-permute-done.2 = f32[32,1024]{1,0:T(8,128)S(1)} collective-permute-done((f32[32,1024]{1,0:T(8,128)S(1)}, f32[32,1024]{1,0:T(8,128)S(1)}, u32[]{:S(2)}, u32[]{:S(2)}) %collective-permute-start.2) | collective-permute-done | bytes 131104 | tf_op jit(solution)/shard_map/ppermute | solution.py:28
  59.2 1.8 %collective-permute-done.3 = f32[32,1024]{1,0:T(8,128)S(1)} collective-permute-done((f32[32,1024]{1,0:T(8,128)S(1)}, f32[32,1024]{1,0:T(8,128)S(1)}, u32[]{:S(2)}, u32[]{:S(2)}) %collective-permute-start.3) | collective-permute-done | bytes 131104 | tf_op jit(solution)/shard_map/ppermute | solution.py:28
  61.0 0.7 %convert_bitcast_fusion = bf16[1,64,1024]{2,1,0:T(8,128)(2,1)} fusion(f32[64,1024]{1,0:T(8,128)S(1)} %fusion.14), kind=kLoop, calls=%fused_computation.22 | loop fusion | flops 65536 | bytes 393216 | tf_op jit(solution)/shard_map/broadcast_in_dim | solution.py:83
  (5 shorter events, 0.1 us)
Async XLA Ops:
  0.0 17.0 %copy-start = (bf16[1024,1024]{1,0:T(8,128)(2,1)S(1)}, bf16[1024,1024]{1,0:T(8,128)(2,1)}, u32[]{:S(2)}) copy-start(bf16[1024,1024]{1,0:T(8,128)(2,1)} %param.18) | copy-start | bytes 6291460
  1.0 16.0 %collective-permute-start = (bf16[32,1024]{1,0:T(8,128)(2,1)S(1)}, bf16[32,1024]{1,0:T(8,128)(2,1)S(1)}, u32[]{:S(2)}, u32[]{:S(2)}) collective-permute-start(bf16[32,1024]{1,0:T(8,128)(2,1)S(1)} %get-tuple-element.31), channel_id=1, source_target_pairs={{0,1},{1,2},{2,3},{3,4},{4,5},{5,6},{6,7},{7,8},{8,9},{9,10},{10,1... | collective-permute-start | bytes 196616 | tf_op jit(solution)/shard_map/ppermute | solution.py:18
  3.0 14.0 %collective-permute-start.1 = (bf16[32,1024]{1,0:T(8,128)(2,1)S(1)}, bf16[32,1024]{1,0:T(8,128)(2,1)S(1)}, u32[]{:S(2)}, u32[]{:S(2)}) collective-permute-start(bf16[32,1024]{1,0:T(8,128)(2,1)S(1)} %get-tuple-element.32), channel_id=1, source_target_pairs={{1,0},{2,1},{3,2},{4,3},{5,4},{6,5},{7,6},{8,7},{9,8},{10,9},{11,1... | collective-permute-start | bytes 196616 | tf_op jit(solution)/shard_map/ppermute | solution.py:21
  17.0 3.8 %copy-start.1 = (bf16[100,1024]{1,0:T(8,128)(2,1)S(1)}, bf16[100,1024]{1,0:T(8,128)(2,1)}, u32[]{:S(2)}) copy-start(bf16[100,1024]{1,0:T(8,128)(2,1)} %param.19) | copy-start | bytes 614404
  23.2 19.4 %copy-start.2 = (f32[512]{0:T(512)S(1)}, f32[512]{0:T(512)}, u32[]{:S(2)}) copy-start(f32[512]{0:T(512)} %param.16) | copy-start | bytes 6148
  24.1 18.0 %all-to-all-start = ((bf16[8,100,512]{2,1,0:T(8,128)(2,1)}), bf16[8,100,512]{2,1,0:T(8,128)(2,1)S(1)}, u32[]{:S(2)}, u32[]{:S(2)}) async-start(bf16[8,100,512]{2,1,0:T(8,128)(2,1)} %broadcast_in_dim.42), calls=%async_computation | async-start | bytes 1703936 | tf_op jit(solution)/shard_map/all_to_all | solution.py:59
  48.9 10.2 %collective-permute-start.2 = (f32[32,1024]{1,0:T(8,128)S(1)}, f32[32,1024]{1,0:T(8,128)S(1)}, u32[]{:S(2)}, u32[]{:S(2)}) collective-permute-start(f32[32,1024]{1,0:T(8,128)S(1)} %get-tuple-element.30), channel_id=1, source_target_pairs={{0,1},{1,2},{2,3},{3,4},{4,5},{5,6},{6,7},{7,8},{8,9},{9,10},{10,1... | collective-permute-start | bytes 393224 | tf_op jit(solution)/shard_map/ppermute | solution.py:28
  50.9 10.1 %collective-permute-start.3 = (f32[32,1024]{1,0:T(8,128)S(1)}, f32[32,1024]{1,0:T(8,128)S(1)}, u32[]{:S(2)}, u32[]{:S(2)}) collective-permute-start(f32[32,1024]{1,0:T(8,128)S(1)} %get-tuple-element.29), channel_id=1, source_target_pairs={{0,63},{1,0},{2,1},{3,2},{4,3},{5,4},{6,5},{7,6},{8,7},{9,8},{10,9... | collective-permute-start | bytes 393224 | tf_op jit(solution)/shard_map/ppermute | solution.py:28

commit v2 on v0

v2 whole, which is shorter than its diff:
```python
import jax
import jax.numpy as jnp
from jax import lax
from jax.experimental import pallas as pl
from jax.experimental.pallas import tpu as pltpu
from jax.sharding import PartitionSpec as P

smooth = 0.0025
bf16 = jnp.bfloat16
f32 = jnp.float32
STEP = 256


def shifted(block, axis, by):
    size = lax.axis_size(axis)
    return lax.ppermute(block, axis, [(i, (i + by) % size) for i in range(size)])


def slope(diff):
    return diff * lax.rsqrt(diff * diff + smooth)


def product(left, right, over):
    return lax.dot_general(left, right, (over, ((), ())), preferred_element_type=f32)


def pack_kernel(mesh_rows, latent, neighbours, live, weight, message):
    rows, half = latent.shape[0], neighbours.shape[1] // 2
    message[:rows] = latent[...]
    first = lax.axis_index("space") * rows
    place = jnp.bitwise_and(neighbours[:, half:] - first, mesh_rows - 1).astype(f32)
    coef = weight[:, half:].astype(f32) * live[:, half:].astype(f32)
    slots = neighbours.shape[0]
    place = jnp.concatenate([place[k : k + 1] for k in range(slots)], axis=1)
    coef = jnp.concatenate([coef[k : k + 1] for k in range(slots)], axis=1)
    row = lax.broadcasted_iota(jnp.int32, (16, place.shape[1]), 0)
    message[rows:] = jnp.where(row == 0, place, jnp.where(row == 1, coef, 0.0)).astype(bf16)


def forward_kernel(
    mesh_rows, message, latent, neighbours, live, weight, w_in, w_out,
    copies, field, gate, adjacency, mixed, hidden,
):
    rows, half = latent.shape[0], neighbours.shape[1] // 2
    slots, channels = neighbours.shape[0], latent.shape[1]
    span = 2 * rows
    row = lax.broadcasted_iota(jnp.int32, (span, half), 0)
    tail = message[rows:].astype(f32)
    first = (lax.axis_index("space") - 1) * rows
    near = jnp.bitwise_and(neighbours[:, :half] - first, mesh_rows - 1)
    near_coef = weight[:, :half].astype(f32) * live[:, :half].astype(f32)
    low = jnp.zeros((span, half), f32)
    high = jnp.zeros((span, half), f32)
    for k in range(slots):
        cut = slice(k * half, (k + 1) * half)
        low = low + jnp.where(row == tail[0:1, cut].astype(jnp.int32), tail[1:2, cut], 0.0)
        high = high + jnp.where(row == near[k : k + 1], near_coef[k : k + 1], 0.0)
    adjacency[:, :half] = low.astype(bf16)
    adjacency[:, half:] = high.astype(bf16)
    edges = adjacency[...]
    twice = jnp.concatenate([edges, edges], axis=0)
    both = jnp.concatenate([message[:rows], latent[...]], axis=0)
    for c in range(0, channels, STEP):
        part = product(both, w_in[:, c : c + STEP], ((1,), (0,)))
        top = part.astype(bf16)
        mixed[:span, c : c + STEP] = top
        mixed[span:, c : c + STEP] = (part - top.astype(f32)).astype(bf16)
    for c in range(0, channels, STEP):
        pre = product(mixed[:, c : c + STEP], twice, ((0,), (0,)))
        sigma = 1.0 / (1.0 + jnp.exp(-pre))
        act = pre * sigma
        hidden[c : c + STEP] = act.astype(bf16)
        gate[c : c + STEP] = sigma + act * (1.0 - sigma)
    out = product(w_out[...], hidden[...], ((1,), (0,)))
    field[...] = out
    rounded = out.astype(bf16)
    for m in range(copies.shape[0]):
        copies[m] = rounded


def backward_kernel(
    every, field, targets, area, moved, gate, adjacency, w_out, w_in, out, rim, joined
):
    members, fields, points = every.shape
    half = points // 2
    rows = out.shape[0]
    me = lax.axis_index("member")
    own = field[...]
    total = jnp.zeros((fields, points), f32)
    for m in range(members):
        total = total + slope(own - every[m].astype(f32)) * jnp.where(me == m, 0.0, 1.0 / (members - 1))
    goal = jnp.concatenate([moved[:fields], targets[:, :half]], axis=1)
    scale = jnp.concatenate([moved[fields : fields + 1], area[:, :half]], axis=1)
    grad_field = (scale * (slope(own - goal) - total)).astype(bf16)
    edges = adjacency[...]
    for c in range(0, gate.shape[0], STEP):
        grad_hidden = product(w_out[:, c : c + STEP], grad_field, ((0,), (0,)))
        grad_pre = (grad_hidden * gate[c : c + STEP]).astype(bf16)
        joined[:, c : c + STEP] = product(edges, grad_pre, ((1,), (1,))).astype(bf16)
    for c in range(0, w_in.shape[0], STEP):
        part = product(joined[...], w_in[c : c + STEP], ((1,), (1,)))
        rim[:, c : c + STEP] = part[:rows].astype(bf16)
        out[:, c : c + STEP] = part[rows:]


def call(kernel, outs, scratch, *operands):
    vmem = pl.BlockSpec(memory_space=pltpu.VMEM)
    return pl.pallas_call(
        kernel,
        out_shape=outs,
        in_specs=[vmem] * len(operands),
        out_specs=[vmem] * len(outs),
        scratch_shapes=scratch,
        compiler_params=pltpu.CompilerParams(vmem_limit_bytes=40 << 20),
    )(*operands)


def per_device(latent, neighbours, live, edge_weight, area, targets, w_in, w_out):
    rows, channels = latent.shape[1:]
    points = neighbours.shape[1]
    fields = targets.shape[0]
    half = points // 2
    mesh_rows = rows * lax.axis_size("space")
    members = lax.axis_size("member")
    span = 2 * rows

    def shape(dims, kind):
        return jax.ShapeDtypeStruct(dims, kind)

    (message,) = call(
        lambda *refs: pack_kernel(mesh_rows, *refs),
        [shape((rows + 16, channels), bf16)],
        [],
        latent[0], neighbours, live, edge_weight,
    )
    received = shifted(message, "space", 1)
    moved = shifted(
        jnp.concatenate([targets[:, half:], area[None, half:]], axis=0), "space", 1
    )
    copies, field, gate, adjacency = call(
        lambda *refs: forward_kernel(mesh_rows, *refs),
        [
            shape((members, fields, points), bf16),
            shape((fields, points), f32),
            shape((channels, points), f32),
            shape((span, points), bf16),
        ],
        [pltpu.VMEM((2 * span, channels), bf16), pltpu.VMEM((channels, points), bf16)],
        received, latent[0], neighbours, live, edge_weight, w_in, w_out,
    )
    every = lax.all_to_all(copies, "member", 0, 0, tiled=True)
    inner, rim = call(
        backward_kernel,
        [shape((rows, channels), f32), shape((rows, channels), bf16)],
        [pltpu.VMEM((span, channels), bf16)],
        every, field, targets, area[None], moved, gate, adjacency, w_out, w_in,
    )
    after = shifted(rim, "space", -1)
    return (inner + after.astype(f32)).astype(bf16)[None]


def solution(mesh):
    return jax.shard_map(
        per_device,
        mesh=mesh,
        in_specs=(
            P("member", "space", None),
            P(None, "space"),
            P(None, "space"),
            P(None, "space"),
            P("space"),
            P(None, "space"),
            P(),
            P(),
        ),
        out_specs=P("member", "space", None),
        check_vma=False,
    )
```

time: 125 us -> 58.9 us (0.47)
  waiting for transfers between devices: 73.5 us -> 14.5 us
  local copies, waits for them, and re-layouts: 1.09 us -> 15.5 us
  between operations: 13.5 us -> 0.13 us
  matrix products: 13 us -> 0 us
  starting transfers between devices: 17 us -> 23.4 us
  other arithmetic: 4.69 us -> 0.69 us
  Pallas kernels: 0 us -> 3.54 us
    all_gather x1 -> x0, waiting for transfers between devices: 68.4 us -> none  [per_device(): every = lax.all_gather(field[None], 'member', axis=0, tiled=True)]
    unnamed x10 -> x42, local copies, waits for them, and re-layouts: 0.02 us -> 15.5 us
    dot_general x4 -> x0, matrix products: 13 us -> none  [the longest x1 3.8 us: per_device(): pre = jnp.dot(joined, w_in, preferred_element_type=jnp.float32)]
    ppermute x4 -> x3, waiting for transfers between devices: 5.02 us -> 14.5 us  [shifted(): lax.ppermute(block, axis, [(i, (i + by) % size) for i in range(size)])]
    all_to_all x0 -> x1, starting transfers between devices: none -> 3.55 us  [per_device(): every = lax.all_to_all(copies, 'member', 0, 0, tiled=True)]
    pallas_call x0 -> x3, Pallas kernels: none -> 3.54 us  [call(): pl.pallas_call(kernel, out_shape=outs, in_specs=[vmem] * len(operands), o...]
    ppermute x4 -> x3, starting transfers between devices: 17 us -> 19.8 us  [shifted(): lax.ppermute(block, axis, [(i, (i + by) % size) for i in range(size)])]
    reduce_sum x2 -> x0, other arithmetic: 2.53 us -> none  [the longest x1 1.81 us: per_device(): pairwise = jnp.sum(slope(field[None] - every), axis=0)]
  transfers between devices with their start and end apart: 5 -> 4, of which waited for: 2 -> 3; matrix products, arithmetic and copies ran while one was open for 2% -> 0% of each run, Pallas kernels for 0% -> 0%
where the time goes in v2:
time: 58.9 us; the launch traced here: 57.7 us
  starting transfers between devices  23.4 us (40%)
  local copies, waits for them, and re-layouts  15.5 us (26%)
  waiting for transfers between devices  14.5 us (25%)
  Pallas kernels  3.54 us (6%)
  other arithmetic  0.69 us (1%)
    ppermute x3, starting transfers between devices, shifted(): lax.ppermute(block, axis, [(i, (i + by) % size) for i in range(size)])  19.8 us
    unnamed x42, local copies, waits for them, and re-layouts  15.5 us
    ppermute x3, waiting for transfers between devices, shifted(): lax.ppermute(block, axis, [(i, (i + by) % size) for i in range(size)])  14.5 us
    all_to_all x1, starting transfers between devices, per_device(): every = lax.all_to_all(copies, 'member', 0, 0, tiled=True)  3.55 us
    pallas_call x3, Pallas kernels, call(): pl.pallas_call(kernel, out_shape=outs, in_specs=[vmem] * len(operands), o...  3.54 us
  transfers between devices with their start and end apart: 4, of which 3 were waited for; matrix products, arithmetic and copies ran while one was open for 0% of the time, Pallas kernels for 0%

profile of v2, /device:TPU:1, one launch (start us, length us, event | category | flops | bytes accessed | tf_op | source)
XLA Modules:
  0.0 57.7 jit_solution(4389330933682239785)
XLA Ops:
  0.0 0.0 copy-start.7
  0.0 0.9 %copy-done.7 = bf16[1,64,1024]{2,1,0:T(8,128)(2,1)S(1)} copy-done((bf16[1,64,1024]{2,1,0:T(8,128)(2,1)S(1)}, bf16[1,64,1024]{2,1,0:T(8,128)(2,1)}, u32[]{:S(2)}) %copy-start.7) | copy-done | bytes 131096
  0.9 0.0 copy-start.14
  0.9 0.7 %copy-done.14 = s32[4,512]{1,0:T(4,128)S(1)} copy-done((s32[4,512]{1,0:T(4,128)S(1)}, s32[4,512]{1,0:T(4,128)}, u32[]{:S(2)}) %copy-start.14) | copy-done | bytes 8216
  1.6 0.0 copy-start.16
  1.6 0.7 %copy-done.16 = s32[4,512]{1,0:T(4,128)S(1)} copy-done((s32[4,512]{1,0:T(4,128)S(1)}, s32[4,512]{1,0:T(4,128)}, u32[]{:S(2)}) %copy-start.16) | copy-done | bytes 8216
  2.3 0.0 copy-start.18
  2.3 0.7 %copy-done.18 = bf16[4,512]{1,0:T(4,128)(2,1)S(1)} copy-done((bf16[4,512]{1,0:T(4,128)(2,1)S(1)}, bf16[4,512]{1,0:T(4,128)(2,1)}, u32[]{:S(2)}) %copy-start.18) | copy-done | bytes 4120
  3.0 0.0 copy-start.20
  3.0 0.0 copy-start.6
  3.0 4.7 %collective-permute-start = (bf16[80,1024]{1,0:T(8,128)(2,1)S(1)}, bf16[80,1024]{1,0:T(8,128)(2,1)S(1)}, u32[]{:S(2)}, u32[]{:S(2)}) collective-permute-start(bf16[80,1024]{1,0:T(8,128)(2,1)S(1)} %shard_map.82), channel_id=1, source_target_pairs={{0,1},{1,2},{2,3},{3,4},{4,5},{5,6},{6,7},{7,8},{8,9},{9,10},{10,1... | collective-permute-start | bytes 491528 | tf_op jit(solution)/shard_map/ppermute | solution.py:16
  7.8 5.1 %collective-permute-done.refs_0_ = bf16[80,1024]{1,0:T(8,128)(2,1)S(1)} collective-permute-done((bf16[80,1024]{1,0:T(8,128)(2,1)S(1)}, bf16[80,1024]{1,0:T(8,128)(2,1)S(1)}, u32[]{:S(2)}, u32[]{:S(2)}) %collective-permute-start) | collective-permute-done | bytes 163872 | tf_op jit(solution)/shard_map/ppermute | solution.py:16
  12.8 0.0 copy-start
  12.8 1.6 %copy-done = bf16[1024,1024]{1,0:T(8,128)(2,1)S(1)} copy-done((bf16[1024,1024]{1,0:T(8,128)(2,1)S(1)}, bf16[1024,1024]{1,0:T(8,128)(2,1)}, u32[]{:S(2)}) %copy-start) | copy-done | bytes 2097176
  14.4 0.0 copy-start.5
  14.4 0.9 %copy-done.5 = bf16[100,1024]{1,0:T(8,128)(2,1)S(1)} copy-done((bf16[100,1024]{1,0:T(8,128)(2,1)S(1)}, bf16[100,1024]{1,0:T(8,128)(2,1)}, u32[]{:S(2)}) %copy-start.5) | copy-done | bytes 204824
  15.3 0.0 copy-start.8
  15.3 0.9 %copy-done.8 = bf16[1,64,1024]{2,1,0:T(8,128)(2,1)S(1)} copy-done((bf16[1,64,1024]{2,1,0:T(8,128)(2,1)S(1)}, bf16[1,64,1024]{2,1,0:T(8,128)(2,1)}, u32[]{:S(2)}) %copy-start.8) | copy-done | bytes 131096
  16.2 0.0 copy-start.15
  16.3 0.7 %copy-done.15 = s32[4,512]{1,0:T(4,128)S(1)} copy-done((s32[4,512]{1,0:T(4,128)S(1)}, s32[4,512]{1,0:T(4,128)}, u32[]{:S(2)}) %copy-start.15) | copy-done | bytes 8216
  16.9 0.0 copy-start.17
  16.9 0.7 %copy-done.17 = s32[4,512]{1,0:T(4,128)S(1)} copy-done((s32[4,512]{1,0:T(4,128)S(1)}, s32[4,512]{1,0:T(4,128)}, u32[]{:S(2)}) %copy-start.17) | copy-done | bytes 8216
  17.6 0.0 copy-start.19
  17.6 0.7 %copy-done.19 = bf16[4,512]{1,0:T(4,128)(2,1)S(1)} copy-done((bf16[4,512]{1,0:T(4,128)(2,1)S(1)}, bf16[4,512]{1,0:T(4,128)(2,1)}, u32[]{:S(2)}) %copy-start.19) | copy-done | bytes 4120
  18.3 0.0 slice-start
  18.3 0.0 copy-start.1
  18.3 0.0 copy-start.9
  18.3 1.5 %shard_map.83 = (bf16[8,100,512]{2,1,0:T(8,128)(2,1)S(1)}, f32[100,512]{1,0:T(8,128)S(1)}, f32[1024,512]{1,0:T(8,128)S(1)}, bf16[128,512]{1,0:T(8,128)(2,1)S(1)}) custom-call(bf16[80,1024]{1,0:T(8,128)(2,1)S(1)} %collective-permute-done.refs_0_, bf16[64,1024]{1,0:T(8,128)(2,1)S(1)} %bitcast.6, s32[4,512]{1,0:T(4,128)S(1)} %copy-done.15, ...), custom_call_target="tpu_custom_call" | custom-call | tf_op jit(solution)/shard_map/pallas_call | solution.py:108
  19.9 0.0 copy-start.2
  19.9 1.3 %copy-done.2 = f32[1024,512]{1,0:T(8,128)} copy-done((f32[1024,512]{1,0:T(8,128)}, f32[1024,512]{1,0:T(8,128)S(1)}, u32[]{:S(2)}) %copy-start.2) | copy-done | bytes 2097176
  21.2 0.0 copy-start.4
  21.2 0.9 %copy-done.4 = bf16[8,100,512]{2,1,0:T(8,128)(2,1)} copy-done((bf16[8,100,512]{2,1,0:T(8,128)(2,1)}, bf16[8,100,512]{2,1,0:T(8,128)(2,1)S(1)}, u32[]{:S(2)}) %copy-start.4) | copy-done | bytes 819224
  22.1 0.0 copy-start.10
  22.1 0.7 %copy-done.10 = f32[100,512]{1,0:T(8,128)} copy-done((f32[100,512]{1,0:T(8,128)}, f32[100,512]{1,0:T(8,128)S(1)}, u32[]{:S(2)}) %copy-start.10) | copy-done | bytes 204824
  22.8 0.0 copy-start.12
  22.8 0.7 %copy-done.12 = bf16[128,512]{1,0:T(8,128)(2,1)} copy-done((bf16[128,512]{1,0:T(8,128)(2,1)}, bf16[128,512]{1,0:T(8,128)(2,1)S(1)}, u32[]{:S(2)}) %copy-start.12) | copy-done | bytes 131096
  23.5 3.5 %all-to-all-start = ((bf16[8,100,512]{2,1,0:T(8,128)(2,1)}), bf16[8,100,512]{2,1,0:T(8,128)(2,1)S(1)}, u32[]{:S(2)}, u32[]{:S(2)}) async-start(bf16[8,100,512]{2,1,0:T(8,128)(2,1)} %copy-done.4), calls=%async_computation | async-start | bytes 1703936 | tf_op jit(solution)/shard_map/all_to_all | solution.py:151
  27.0 0.0 copy-done.20
  27.0 0.0 slice-done
  27.1 4.0 %collective-permute-start.1 = (f32[101,256]{1,0:T(8,128)S(1)}, f32[101,256]{1,0:T(8,128)S(1)}, u32[]{:S(2)}, u32[]{:S(2)}) collective-permute-start(f32[101,256]{1,0:T(8,128)S(1)} %pad_maximum_fusion), channel_id=1, source_target_pairs={{0,1},{1,2},{2,3},{3,4},{4,5},{5,6},{6,7},{7,8},{8,9},{9,10},{10,1... | collective-permute-start | bytes 310280 | tf_op jit(solution)/shard_map/ppermute | solution.py:16
  31.1 8.4 %collective-permute-done.1.moved = f32[101,256]{1,0:T(8,128)S(1)} collective-permute-done((f32[101,256]{1,0:T(8,128)S(1)}, f32[101,256]{1,0:T(8,128)S(1)}, u32[]{:S(2)}, u32[]{:S(2)}) %collective-permute-start.1) | collective-permute-done | bytes 103456 | tf_op jit(solution)/shard_map/ppermute | solution.py:16
  39.5 0.0 all-to-all-done.every
  39.5 0.0 copy-done.6
  39.5 0.0 copy-done.1
  39.5 0.0 copy-done.9
  39.6 0.0 copy-start.3
  39.6 1.6 %copy-done.3 = f32[1024,512]{1,0:T(8,128)S(1)} copy-done((f32[1024,512]{1,0:T(8,128)S(1)}, f32[1024,512]{1,0:T(8,128)}, u32[]{:S(2)}) %copy-start.3) | copy-done | bytes 2097176
  41.1 0.0 copy-start.11
  41.1 0.9 %copy-done.11 = f32[100,512]{1,0:T(8,128)S(1)} copy-done((f32[100,512]{1,0:T(8,128)S(1)}, f32[100,512]{1,0:T(8,128)}, u32[]{:S(2)}) %copy-start.11) | copy-done | bytes 204824
  42.1 0.0 copy-start.13
  42.1 0.9 %copy-done.13 = bf16[128,512]{1,0:T(8,128)(2,1)S(1)} copy-done((bf16[128,512]{1,0:T(8,128)(2,1)S(1)}, bf16[128,512]{1,0:T(8,128)(2,1)}, u32[]{:S(2)}) %copy-start.13) | copy-done | bytes 131096
  43.0 2.0 %shard_map.84 = (f32[64,1024]{1,0:T(8,128)S(1)}, bf16[64,1024]{1,0:T(8,128)(2,1)S(1)}) custom-call(bf16[8,100,512]{2,1,0:T(8,128)(2,1)S(1)} %all-to-all-done.every, f32[100,512]{1,0:T(8,128)S(1)} %copy-done.11, f32[100,512]{1,0:T(8,128)S(1)} %copy-done.9, f32[1,512]{1,0:T(1,128)S(1)} %bitcast.7, f32[101,256]{1,0:T(8,128)S(1)} %collective-permute-done.1.moved, ...), custom_call_target="tpu_custom_call" | custom-call | tf_op jit(solution)/shard_map/pallas_call | solution.py:108
  45.0 11.1 %collective-permute-start.2 = (bf16[64,1024]{1,0:T(8,128)(2,1)S(1)}, bf16[64,1024]{1,0:T(8,128)(2,1)S(1)}, u32[]{:S(2)}, u32[]{:S(2)}) collective-permute-start(bf16[64,1024]{1,0:T(8,128)(2,1)S(1)} %get-tuple-element.16), channel_id=1, source_target_pairs={{0,63},{1,0},{2,1},{3,2},{4,3},{5,4},{6,5},{7,6},{8,7},{9,8},{10,9... | collective-permute-start | bytes 393224 | tf_op jit(solution)/shard_map/ppermute | solution.py:16
  56.1 1.0 %collective-permute-done.2 = bf16[64,1024]{1,0:T(8,128)(2,1)S(1)} collective-permute-done((bf16[64,1024]{1,0:T(8,128)(2,1)S(1)}, bf16[64,1024]{1,0:T(8,128)(2,1)S(1)}, u32[]{:S(2)}, u32[]{:S(2)}) %collective-permute-start.2) | collective-permute-done | bytes 131104 | tf_op jit(solution)/shard_map/ppermute | solution.py:16
  57.0 0.7 %fusion = bf16[1,64,1024]{2,1,0:T(8,128)(2,1)} fusion(f32[64,1024]{1,0:T(8,128)S(1)} %get-tuple-element.15, bf16[64,1024]{1,0:T(8,128)(2,1)S(1)} %collective-permute-done.2), kind=kLoop, calls=%fused_computation.1 | loop fusion | flops 196608 | bytes 524288 | tf_op jit(solution)/shard_map/broadcast_in_dim | solution.py:159
  (3 shorter events, 0.0 us)
Async XLA Ops:
  0.0 0.9 %copy-start.7 = (bf16[1,64,1024]{2,1,0:T(8,128)(2,1)S(1)}, bf16[1,64,1024]{2,1,0:T(8,128)(2,1)}, u32[]{:S(2)}) copy-start(bf16[1,64,1024]{2,1,0:T(8,128)(2,1)} %param.8) | copy-start | bytes 393220
  0.9 0.7 %copy-start.14 = (s32[4,512]{1,0:T(4,128)S(1)}, s32[4,512]{1,0:T(4,128)}, u32[]{:S(2)}) copy-start(s32[4,512]{1,0:T(4,128)} %refs_2_.3) | copy-start | bytes 24580
  1.6 0.7 %copy-start.16 = (s32[4,512]{1,0:T(4,128)S(1)}, s32[4,512]{1,0:T(4,128)}, u32[]{:S(2)}) copy-start(s32[4,512]{1,0:T(4,128)} %refs_3_.3) | copy-start | bytes 24580
  2.3 0.7 %copy-start.18 = (bf16[4,512]{1,0:T(4,128)(2,1)S(1)}, bf16[4,512]{1,0:T(4,128)(2,1)}, u32[]{:S(2)}) copy-start(bf16[4,512]{1,0:T(4,128)(2,1)} %refs_4_.1) | copy-start | bytes 12292
  3.0 24.0 %copy-start.20 = (f32[512]{0:T(512)S(1)}, f32[512]{0:T(512)}, u32[]{:S(2)}) copy-start(f32[512]{0:T(512)} %param.12) | copy-start | bytes 6148
  3.0 36.5 %copy-start.6 = (bf16[100,1024]{1,0:T(8,128)(2,1)S(1)}, bf16[100,1024]{1,0:T(8,128)(2,1)}, u32[]{:S(2)}) copy-start(bf16[100,1024]{1,0:T(8,128)(2,1)} %w_out.1) | copy-start | bytes 614404
  3.0 9.8 %collective-permute-start = (bf16[80,1024]{1,0:T(8,128)(2,1)S(1)}, bf16[80,1024]{1,0:T(8,128)(2,1)S(1)}, u32[]{:S(2)}, u32[]{:S(2)}) collective-permute-start(bf16[80,1024]{1,0:T(8,128)(2,1)S(1)} %shard_map.82), channel_id=1, source_target_pairs={{0,1},{1,2},{2,3},{3,4},{4,5},{5,6},{6,7},{7,8},{8,9},{9,10},{10,1... | collective-permute-start | bytes 491528 | tf_op jit(solution)/shard_map/ppermute | solution.py:16
  12.8 1.6 %copy-start = (bf16[1024,1024]{1,0:T(8,128)(2,1)S(1)}, bf16[1024,1024]{1,0:T(8,128)(2,1)}, u32[]{:S(2)}) copy-start(bf16[1024,1024]{1,0:T(8,128)(2,1)} %w_in.1) | copy-start | bytes 6291460
  14.4 0.9 %copy-start.5 = (bf16[100,1024]{1,0:T(8,128)(2,1)S(1)}, bf16[100,1024]{1,0:T(8,128)(2,1)}, u32[]{:S(2)}) copy-start(bf16[100,1024]{1,0:T(8,128)(2,1)} %w_out.1) | copy-start | bytes 614404
  15.3 0.9 %copy-start.8 = (bf16[1,64,1024]{2,1,0:T(8,128)(2,1)S(1)}, bf16[1,64,1024]{2,1,0:T(8,128)(2,1)}, u32[]{:S(2)}) copy-start(bf16[1,64,1024]{2,1,0:T(8,128)(2,1)} %param.8) | copy-start | bytes 393220
  16.2 0.7 %copy-start.15 = (s32[4,512]{1,0:T(4,128)S(1)}, s32[4,512]{1,0:T(4,128)}, u32[]{:S(2)}) copy-start(s32[4,512]{1,0:T(4,128)} %refs_2_.3) | copy-start | bytes 24580
  16.9 0.7 %copy-start.17 = (s32[4,512]{1,0:T(4,128)S(1)}, s32[4,512]{1,0:T(4,128)}, u32[]{:S(2)}) copy-start(s32[4,512]{1,0:T(4,128)} %refs_3_.3) | copy-start | bytes 24580
  17.6 0.7 %copy-start.19 = (bf16[4,512]{1,0:T(4,128)(2,1)S(1)}, bf16[4,512]{1,0:T(4,128)(2,1)}, u32[]{:S(2)}) copy-start(bf16[4,512]{1,0:T(4,128)(2,1)} %refs_4_.1) | copy-start | bytes 12292
  18.3 8.7 %slice-start = ((f32[100,512]{1,0:T(8,128)}), f32[100,256]{1,0:T(8,128)S(1)}, s32[]{:S(2)}) async-start(f32[100,512]{1,0:T(8,128)} %targets.1), calls=%async_computation.1 | async-start | bytes 212992 | tf_op jit(solution)/shard_map/slice | solution.py:138
  18.3 21.2 %copy-start.1 = (bf16[1024,1024]{1,0:T(8,128)(2,1)S(1)}, bf16[1024,1024]{1,0:T(8,128)(2,1)}, u32[]{:S(2)}) copy-start(bf16[1024,1024]{1,0:T(8,128)(2,1)} %w_in.1) | copy-start | bytes 6291460
  18.3 21.2 %copy-start.9 = (f32[100,512]{1,0:T(8,128)S(1)}, f32[100,512]{1,0:T(8,128)}, u32[]{:S(2)}) copy-start(f32[100,512]{1,0:T(8,128)} %targets.1) | copy-start | bytes 614404
  19.9 1.3 %copy-start.2 = (f32[1024,512]{1,0:T(8,128)}, f32[1024,512]{1,0:T(8,128)S(1)}, u32[]{:S(2)}) copy-start(f32[1024,512]{1,0:T(8,128)S(1)} %get-tuple-element.13.gate) | copy-start | bytes 6291460
  21.2 0.9 %copy-start.4 = (bf16[8,100,512]{2,1,0:T(8,128)(2,1)}, bf16[8,100,512]{2,1,0:T(8,128)(2,1)S(1)}, u32[]{:S(2)}) copy-start(bf16[8,100,512]{2,1,0:T(8,128)(2,1)S(1)} %get-tuple-element.11) | copy-start | bytes 2457604
  22.1 0.7 %copy-start.10 = (f32[100,512]{1,0:T(8,128)}, f32[100,512]{1,0:T(8,128)S(1)}, u32[]{:S(2)}) copy-start(f32[100,512]{1,0:T(8,128)S(1)} %get-tuple-element.12.field) | copy-start | bytes 614404
  22.8 0.7 %copy-start.12 = (bf16[128,512]{1,0:T(8,128)(2,1)}, bf16[128,512]{1,0:T(8,128)(2,1)S(1)}, u32[]{:S(2)}) copy-start(bf16[128,512]{1,0:T(8,128)(2,1)S(1)} %get-tuple-element.14.adjacency) | copy-start | bytes 393220
  23.5 16.1 %all-to-all-start = ((bf16[8,100,512]{2,1,0:T(8,128)(2,1)}), bf16[8,100,512]{2,1,0:T(8,128)(2,1)S(1)}, u32[]{:S(2)}, u32[]{:S(2)}) async-start(bf16[8,100,512]{2,1,0:T(8,128)(2,1)} %copy-done.4), calls=%async_computation | async-start | bytes 1703936 | tf_op jit(solution)/shard_map/all_to_all | solution.py:151
  27.1 12.5 %collective-permute-start.1 = (f32[101,256]{1,0:T(8,128)S(1)}, f32[101,256]{1,0:T(8,128)S(1)}, u32[]{:S(2)}, u32[]{:S(2)}) collective-permute-start(f32[101,256]{1,0:T(8,128)S(1)} %pad_maximum_fusion), channel_id=1, source_target_pairs={{0,1},{1,2},{2,3},{3,4},{4,5},{5,6},{6,7},{7,8},{8,9},{9,10},{10,1... | collective-permute-start | bytes 310280 | tf_op jit(solution)/shard_map/ppermute | solution.py:16
  39.6 1.6 %copy-start.3 = (f32[1024,512]{1,0:T(8,128)S(1)}, f32[1024,512]{1,0:T(8,128)}, u32[]{:S(2)}) copy-start(f32[1024,512]{1,0:T(8,128)} %copy-done.2) | copy-start | bytes 6291460
  41.1 0.9 %copy-start.11 = (f32[100,512]{1,0:T(8,128)S(1)}, f32[100,512]{1,0:T(8,128)}, u32[]{:S(2)}) copy-start(f32[100,512]{1,0:T(8,128)} %copy-done.10) | copy-start | bytes 614404
  42.1 0.9 %copy-start.13 = (bf16[128,512]{1,0:T(8,128)(2,1)S(1)}, bf16[128,512]{1,0:T(8,128)(2,1)}, u32[]{:S(2)}) copy-start(bf16[128,512]{1,0:T(8,128)(2,1)} %copy-done.12) | copy-start | bytes 393220
  45.0 12.1 %collective-permute-start.2 = (bf16[64,1024]{1,0:T(8,128)(2,1)S(1)}, bf16[64,1024]{1,0:T(8,128)(2,1)S(1)}, u32[]{:S(2)}, u32[]{:S(2)}) collective-permute-start(bf16[64,1024]{1,0:T(8,128)(2,1)S(1)} %get-tuple-element.16), channel_id=1, source_target_pairs={{0,63},{1,0},{2,1},{3,2},{4,3},{5,4},{6,5},{7,6},{8,7},{9,8},{10,9... | collective-permute-start | bytes 393224 | tf_op jit(solution)/shard_map/ppermute | solution.py:16

commit v3 on v2

v3 whole, which is shorter than its diff:
```python
import jax
import jax.numpy as jnp
from jax import lax
from jax.experimental import pallas as pl
from jax.experimental.pallas import tpu as pltpu
from jax.sharding import PartitionSpec as P

smooth = 0.0025
bf16 = jnp.bfloat16
f32 = jnp.float32
STEP = 256
LIMITS = (48, 48, 48)
KEPT = 16640


def shifted(block, axis, by):
    size = lax.axis_size(axis)
    return lax.ppermute(block, axis, [(i, (i + by) % size) for i in range(size)])


def slope(diff):
    return diff * lax.rsqrt(diff * diff + smooth)


def product(left, right, over):
    return lax.dot_general(left, right, (over, ((), ())), preferred_element_type=f32)


def adjacent(span, edges):
    slots, half = edges.shape[0] // 2, edges.shape[1]
    row = lax.broadcasted_iota(jnp.int32, (span, half), 0)
    total = jnp.zeros((span, half), f32)
    for k in range(slots):
        place = edges[k : k + 1].astype(jnp.int32)
        total = total + jnp.where(row == place, edges[slots + k : slots + k + 1], 0.0)
    return total.astype(bf16)


def halves(part):
    top = part.astype(bf16)
    return top, (part - top.astype(f32)).astype(bf16)


def own_kernel(message, w_in, own_top, own_rest, own_edges):
    rows, channels = own_top.shape
    span, half = own_edges.shape
    tail = message[rows:, :half].astype(f32)
    own_edges[...] = adjacent(span, tail[tail.shape[0] // 2 :])
    for c in range(0, channels, STEP):
        cut = slice(c, c + STEP)
        part = product(message[:rows], w_in[:, cut], ((1,), (0,)))
        own_top[:, cut], own_rest[:, cut] = halves(part)


def forward_kernel(
    message, own_top, own_rest, own_edges, w_in, w_out, copies, kept,
    mixed, hidden, rounded, gates, edges, wide, done,
):
    rows, channels = own_top.shape
    span, half = own_edges.shape
    members, count, points = copies.shape
    sent = []

    def send(source, target):
        copy = pltpu.make_async_copy(source, target, done.at[len(sent)])
        copy.start()
        sent.append(copy)

    tail = message[rows:, :half].astype(f32)
    edges[:, :half] = adjacent(span, tail[: tail.shape[0] // 2])
    edges[:, half:] = own_edges[...]
    send(edges, kept.at[pl.ds(channels, span)])
    both = edges[...]
    twice = jnp.concatenate([both, both], axis=0)
    for c in range(0, channels, STEP):
        cut = slice(c, c + STEP)
        part = product(message[:rows], w_in[:, cut], ((1,), (0,)))
        mixed[:rows, cut], mixed[span : span + rows, cut] = halves(part)
    mixed[rows:span] = own_top[...]
    mixed[span + rows :] = own_rest[...]
    for c in range(0, channels, STEP):
        cut = slice(c, c + STEP)
        pre = product(mixed[:, cut], twice, ((0,), (0,)))
        sigma = 1.0 / (1.0 + jnp.exp(-pre))
        act = pre * sigma
        hidden[cut] = act.astype(bf16)
        gates[cut] = (sigma + act * (1.0 - sigma)).astype(bf16)
        send(gates.at[pl.ds(c, STEP)], kept.at[pl.ds(c, STEP)])
    out = product(w_out[...], hidden[...], ((1,), (0,)))
    rounded[...] = out.astype(bf16)
    for m in range(members):
        send(rounded, copies.at[m])
    room = wide.shape[0] // 2
    padded = jnp.concatenate([out, jnp.zeros((room - count, points), f32)], axis=0)
    wide[:room], wide[room:] = halves(padded)
    send(wide, kept.at[pl.ds(channels + span, 2 * room)])
    for copy in sent:
        copy.wait()


def backward_kernel(
    every, moved, targets, area, w_out, w_in, kept, out, rim,
    joined, gates, edges, wide, done,
):
    members, count, points = every.shape
    half = points // 2
    rows, channels = out.shape
    span = 2 * rows
    room = wide.shape[0] // 2
    loads = [(kept.at[pl.ds(channels + span, 2 * room)], wide)]
    loads += [(kept.at[pl.ds(c, STEP)], gates.at[pl.ds(c, STEP)]) for c in range(0, channels, STEP)]
    loads += [(kept.at[pl.ds(channels, span)], edges)]
    loads = [pltpu.make_async_copy(*pair, done.at[i]) for i, pair in enumerate(loads)]
    for copy in loads:
        copy.start()
    me = lax.axis_index("member")
    loads[0].wait()
    own = (wide[:room].astype(f32) + wide[room:].astype(f32))[:count]
    total = jnp.zeros((count, points), f32)
    for m in range(members):
        total = total + slope(own - every[m].astype(f32)) * jnp.where(me == m, 0.0, 1.0 / (members - 1))
    goal = jnp.concatenate([moved[:count], targets[:, :half]], axis=1)
    scale = jnp.concatenate([moved[count : count + 1], area[:, :half]], axis=1)
    grad_field = (scale * (slope(own - goal) - total)).astype(bf16)
    for copy in loads[1:]:
        copy.wait()
    for c in range(0, channels, STEP):
        cut = slice(c, c + STEP)
        grad_hidden = product(w_out[:, cut], grad_field, ((0,), (0,)))
        grad_pre = (grad_hidden * gates[cut].astype(f32)).astype(bf16)
        joined[:, cut] = product(edges[...], grad_pre, ((1,), (1,))).astype(bf16)
    for c in range(0, channels, STEP):
        cut = slice(c, c + STEP)
        part = product(joined[...], w_in[cut], ((1,), (1,)))
        rim[:, cut] = part[:rows].astype(bf16)
        out[:, cut] = part[rows:]


HERE = pl.BlockSpec(memory_space=pltpu.VMEM)
AWAY = pl.BlockSpec(memory_space=pl.ANY)


def call(kernel, limit, ins, outs, scratch, copies=0):
    return pl.pallas_call(
        kernel,
        out_shape=[jax.ShapeDtypeStruct(dims, kind) for _, dims, kind in outs],
        in_specs=[spec for spec, _ in ins],
        out_specs=[spec for spec, _, _ in outs],
        scratch_shapes=[pltpu.VMEM(dims, kind) for dims, kind in scratch]
        + [pltpu.SemaphoreType.DMA((copies,))] * (copies > 0),
        compiler_params=pltpu.CompilerParams(vmem_limit_bytes=limit << 20),
        cost_estimate=pl.CostEstimate(flops=10**10, bytes_accessed=4 << 20, transcendentals=0),
    )(*[operand for _, operand in ins])


def per_device(latent, neighbours, live, edge_weight, area, targets, w_in, w_out):
    rows, channels = latent.shape[1:]
    slots, points = neighbours.shape
    fields = targets.shape[0]
    half = points // 2
    mesh_rows = rows * lax.axis_size("space")
    members = lax.axis_size("member")
    span = 2 * rows
    room = -(-fields // 16) * 16

    first = lax.axis_index("space") * rows
    coef = edge_weight * live.astype(bf16)
    high = jnp.bitwise_and(neighbours[:, half:] - first, mesh_rows - 1).astype(bf16)
    low = jnp.bitwise_and(neighbours[:, :half] - (first - rows), mesh_rows - 1).astype(bf16)
    tail = jnp.concatenate([high, coef[:, half:], low, coef[:, :half]], axis=0)
    message = jnp.concatenate([latent[0], jnp.pad(tail, ((0, 0), (0, channels - half)))], axis=0)
    received = shifted(message, "space", 1)
    own_top, own_rest, own_edges = call(
        own_kernel,
        LIMITS[0],
        [(HERE, message), (HERE, w_in)],
        [(HERE, (rows, channels), bf16), (HERE, (rows, channels), bf16), (HERE, (span, half), bf16)],
        [],
    )
    moved = shifted(
        jnp.concatenate([targets[:, half:], area[None, half:]], axis=0), "space", 1
    )
    copies, kept = call(
        forward_kernel,
        LIMITS[1],
        [(HERE, x) for x in (received, own_top, own_rest, own_edges, w_in, w_out)],
        [
            (AWAY, (members, fields, points), bf16),
            (AWAY, (KEPT, points), bf16),
        ],
        [
            ((2 * span, channels), bf16),
            ((channels, points), bf16),
            ((fields, points), bf16),
            ((channels, points), bf16),
            ((span, points), bf16),
            ((2 * room, points), bf16),
        ],
        members + channels // STEP + 2,
    )
    every = lax.all_to_all(copies, "member", 0, 0, tiled=True)
    inner, rim = call(
        backward_kernel,
        LIMITS[2],
        [(HERE, x) for x in (every, moved, targets, area[None], w_out, w_in)] + [(AWAY, kept)],
        [(HERE, (rows, channels), f32), (HERE, (rows, channels), bf16)],
        [
            ((span, channels), bf16),
            ((channels, points), bf16),
            ((span, points), bf16),
            ((2 * room, points), bf16),
        ],
        channels // STEP + 2,
    )
    after = shifted(rim, "space", -1)
    return (inner + after.astype(f32)).astype(bf16)[None]


def solution(mesh):
    return jax.shard_map(
        per_device,
        mesh=mesh,
        in_specs=(
            P("member", "space", None),
            P(None, "space"),
            P(None, "space"),
            P(None, "space"),
            P("space"),
            P(None, "space"),
            P(),
            P(),
        ),
        out_specs=P("member", "space", None),
        check_vma=False,
    )
```

time: 58.9 us -> 48 us (0.81)
  the two profiles are of different devices: /device:TPU:1 before, /device:TPU:4 now
where the time goes in v3:
time: 48 us; the launch traced here: 47.6 us
  waiting for transfers between devices  20.6 us (43%)
  starting transfers between devices  15.8 us (33%)
  Pallas kernels  6.45 us (13%)
  other arithmetic  3.06 us (6%)
  local copies, waits for them, and re-layouts  1.62 us (3%)
    ppermute x3, waiting for transfers between devices, shifted(): lax.ppermute(block, axis, [(i, (i + by) % size) for i in range(size)])  19.5 us
    ppermute x3, starting transfers between devices, shifted(): lax.ppermute(block, axis, [(i, (i + by) % size) for i in range(size)])  8.69 us
    all_to_all x1, starting transfers between devices, per_device(): every = lax.all_to_all(copies, 'member', 0, 0, tiled=True)  7.14 us
    pallas_call x3, Pallas kernels, call(): pl.pallas_call(kernel, out_shape=[jax.ShapeDtypeStruct(dims, kind) for _,...  6.45 us
    unnamed x10, local copies, waits for them, and re-layouts  1.6 us
    all_to_all x1, waiting for transfers between devices, per_device(): every = lax.all_to_all(copies, 'member', 0, 0, tiled=True)  1.11 us
  transfers between devices with their start and end apart: 4, of which 4 were waited for; matrix products, arithmetic and copies ran while one was open for 0% of the time, Pallas kernels for 1%

profile of v3, /device:TPU:4, one launch (start us, length us, event | category | flops | bytes accessed | tf_op | source)
XLA Modules:
  0.0 47.6 jit_solution(10784954412804156562)
XLA Ops:
  0.0 0.7 %convert_multiply_fusion = bf16[4,512]{1,0:T(4,128)(2,1)S(1)} fusion(bf16[4,512]{1,0:T(4,128)(2,1)} %param.11, s32[4,512]{1,0:T(4,128)} %param.10), kind=kLoop, calls=%fused_computation.13 | loop fusion | flops 4096 | bytes 16384 | tf_op jit(solution)/shard_map/mul | solution.py:167
  0.7 0.7 %and_convert_fusion.1 = (bf16[4,256]{1,0:T(4,128)(2,1)S(1)}, bf16[4,256]{1,0:T(4,128)(2,1)S(1)}) fusion(s32[4,512]{1,0:T(4,128)} %param.9, s32[]{:T(128)S(6)} %mul.6, s32[]{:T(128)S(6)} %sub.17), kind=kLoop, calls=%fused_computation.14 | loop fusion | flops 6144 | bytes 12296 | tf_op jit(solution)/shard_map/convert_element_type | solution.py:168
  1.5 0.9 %pad_maximum_fusion.message = bf16[80,1024]{1,0:T(8,128)(2,1)S(1)} fusion(bf16[16,1024]{1,0:T(8,128)(2,1)S(1)} %fusion.7, bf16[64,1024]{1,0:T(8,128)(2,1)} %bitcast.6), kind=kLoop, calls=%fused_computation.1 | loop fusion | flops 327680 | bytes 327680 | tf_op jit(solution)/shard_map/concatenate | solution.py:171
  2.4 1.9 %collective-permute-start = (bf16[80,1024]{1,0:T(8,128)(2,1)S(1)}, bf16[80,1024]{1,0:T(8,128)(2,1)S(1)}, u32[]{:S(2)}, u32[]{:S(2)}) collective-permute-start(bf16[80,1024]{1,0:T(8,128)(2,1)S(1)} %pad_maximum_fusion.message), channel_id=1, source_target_pairs={{0,1},{1,2},{2,3},{3,4},{4,5},{5,6},{6,7},{7,8},{8,9},{9,10},{10,1... | collective-permute-start | bytes 491528 | tf_op jit(solution)/shard_map/ppermute | solution.py:18
  4.3 0.0 copy-start.2
  4.3 1.6 %copy-done.2 = bf16[1024,1024]{1,0:T(8,128)(2,1)S(1)} copy-done((bf16[1024,1024]{1,0:T(8,128)(2,1)S(1)}, bf16[1024,1024]{1,0:T(8,128)(2,1)}, u32[]{:S(2)}) %copy-start.2) | copy-done | bytes 2097176
  5.9 0.0 copy-start.4
  5.9 0.6 %shard_map.82 = (bf16[64,1024]{1,0:T(8,128)(2,1)S(1)}, bf16[64,1024]{1,0:T(8,128)(2,1)S(1)}, bf16[128,256]{1,0:T(8,128)(2,1)S(1)}) custom-call(bf16[80,1024]{1,0:T(8,128)(2,1)S(1)} %pad_maximum_fusion.message, bf16[1024,1024]{1,0:T(8,128)(2,1)S(1)} %copy-done.2), custom_call_target="tpu_custom_call" | custom-call | flops 10000000000 | bytes 4194304 | tf_op jit(solution)/shard_map/pallas_call | solution.py:144
  6.5 10.8 %collective-permute-done.message = bf16[80,1024]{1,0:T(8,128)(2,1)S(1)} collective-permute-done((bf16[80,1024]{1,0:T(8,128)(2,1)S(1)}, bf16[80,1024]{1,0:T(8,128)(2,1)S(1)}, u32[]{:S(2)}, u32[]{:S(2)}) %collective-permute-start) | collective-permute-done | bytes 163872 | tf_op jit(solution)/shard_map/ppermute | solution.py:18
  17.2 0.0 copy-done.4
  17.2 0.0 copy-start.1
  17.2 0.0 slice-start
  17.2 0.0 copy-start
  17.2 0.0 copy-start.3
  17.3 2.7 %shard_map.83 = (bf16[8,100,512]{2,1,0:T(8,128)(2,1)}, bf16[16640,512]{1,0:T(8,128)(2,1)}) custom-call(bf16[80,1024]{1,0:T(8,128)(2,1)S(1)} %collective-permute-done.message, bf16[64,1024]{1,0:T(8,128)(2,1)S(1)} %get-tuple-element.12.own_top, bf16[64,1024]{1,0:T(8,128)(2,1)S(1)} %get-tuple-element.13.own_rest, ...), custom_call_target="tpu_custom_call" | custom-call | flops 10000000000 | bytes 4194304 | tf_op jit(solution)/shard_map/pallas_call | solution.py:144
  20.0 7.1 %all-to-all-start = ((bf16[8,100,512]{2,1,0:T(8,128)(2,1)}), bf16[8,100,512]{2,1,0:T(8,128)(2,1)S(1)}, u32[]{:S(2)}, u32[]{:S(2)}) async-start(bf16[8,100,512]{2,1,0:T(8,128)(2,1)} %get-tuple-element.15), calls=%async_computation | async-start | bytes 1703936 | tf_op jit(solution)/shard_map/all_to_all | solution.py:201
  27.1 0.0 copy-done.1
  27.1 0.0 slice-done
  27.1 1.9 %collective-permute-start.1 = (f32[101,256]{1,0:T(8,128)S(1)}, f32[101,256]{1,0:T(8,128)S(1)}, u32[]{:S(2)}, u32[]{:S(2)}) collective-permute-start(f32[101,256]{1,0:T(8,128)S(1)} %pad_maximum_fusion.1), channel_id=1, source_target_pairs={{0,1},{1,2},{2,3},{3,4},{4,5},{5,6},{6,7},{7,8},{8,9},{9,10},{10,1... | collective-permute-start | bytes 310280 | tf_op jit(solution)/shard_map/ppermute | solution.py:18
  29.1 6.2 %collective-permute-done.1.moved = f32[101,256]{1,0:T(8,128)S(1)} collective-permute-done((f32[101,256]{1,0:T(8,128)S(1)}, f32[101,256]{1,0:T(8,128)S(1)}, u32[]{:S(2)}, u32[]{:S(2)}) %collective-permute-start.1) | collective-permute-done | bytes 103456 | tf_op jit(solution)/shard_map/ppermute | solution.py:18
  35.3 1.1 %all-to-all-done.every = bf16[8,100,512]{2,1,0:T(8,128)(2,1)S(1)} async-done(((bf16[8,100,512]{2,1,0:T(8,128)(2,1)}), bf16[8,100,512]{2,1,0:T(8,128)(2,1)S(1)}, u32[]{:S(2)}, u32[]{:S(2)}) %all-to-all-start) | async-done | bytes 819232 | tf_op jit(solution)/shard_map/all_to_all | solution.py:201
  36.4 0.0 copy-done
  36.4 0.0 copy-done.3
  36.4 3.2 %shard_map.84 = (f32[64,1024]{1,0:T(8,128)S(1)}, bf16[64,1024]{1,0:T(8,128)(2,1)S(1)}) custom-call(bf16[8,100,512]{2,1,0:T(8,128)(2,1)S(1)} %all-to-all-done.every, f32[101,256]{1,0:T(8,128)S(1)} %collective-permute-done.1.moved, f32[100,512]{1,0:T(8,128)S(1)} %copy-done, f32[1,512]{1,0:T(1,128)S(1)} %bitcast.5, bf16[100,1024]{1,0:T(8,128)(2,1)S(1)} %copy-done.4, ...), custom_call_target="tpu_custom_call" | custom-call | flops 10000000000 | bytes 4194304 | tf_op jit(solution)/shard_map/pallas_call | solution.py:144
  39.6 4.8 %collective-permute-start.2 = (bf16[64,1024]{1,0:T(8,128)(2,1)S(1)}, bf16[64,1024]{1,0:T(8,128)(2,1)S(1)}, u32[]{:S(2)}, u32[]{:S(2)}) collective-permute-start(bf16[64,1024]{1,0:T(8,128)(2,1)S(1)} %get-tuple-element.18), channel_id=1, source_target_pairs={{0,63},{1,0},{2,1},{3,2},{4,3},{5,4},{6,5},{7,6},{8,7},{9,8},{10,9... | collective-permute-start | bytes 393224 | tf_op jit(solution)/shard_map/ppermute | solution.py:18
  44.4 2.5 %collective-permute-done.2 = bf16[64,1024]{1,0:T(8,128)(2,1)S(1)} collective-permute-done((bf16[64,1024]{1,0:T(8,128)(2,1)S(1)}, bf16[64,1024]{1,0:T(8,128)(2,1)S(1)}, u32[]{:S(2)}, u32[]{:S(2)}) %collective-permute-start.2) | collective-permute-done | bytes 131104 | tf_op jit(solution)/shard_map/ppermute | solution.py:18
  46.9 0.7 %fusion = bf16[1,64,1024]{2,1,0:T(8,128)(2,1)} fusion(f32[64,1024]{1,0:T(8,128)S(1)} %get-tuple-element.17, bf16[64,1024]{1,0:T(8,128)(2,1)S(1)} %collective-permute-done.2), kind=kLoop, calls=%fused_computation.2 | loop fusion | flops 196608 | bytes 524288 | tf_op jit(solution)/shard_map/broadcast_in_dim | solution.py:216
  (4 shorter events, 0.0 us)
Async XLA Ops:
  2.4 14.9 %collective-permute-start = (bf16[80,1024]{1,0:T(8,128)(2,1)S(1)}, bf16[80,1024]{1,0:T(8,128)(2,1)S(1)}, u32[]{:S(2)}, u32[]{:S(2)}) collective-permute-start(bf16[80,1024]{1,0:T(8,128)(2,1)S(1)} %pad_maximum_fusion.message), channel_id=1, source_target_pairs={{0,1},{1,2},{2,3},{3,4},{4,5},{5,6},{6,7},{7,8},{8,9},{9,10},{10,1... | collective-permute-start | bytes 491528 | tf_op jit(solution)/shard_map/ppermute | solution.py:18
  4.3 1.6 %copy-start.2 = (bf16[1024,1024]{1,0:T(8,128)(2,1)S(1)}, bf16[1024,1024]{1,0:T(8,128)(2,1)}, u32[]{:S(2)}) copy-start(bf16[1024,1024]{1,0:T(8,128)(2,1)} %w_in.5) | copy-start | bytes 6291460
  5.9 11.3 %copy-start.4 = (bf16[100,1024]{1,0:T(8,128)(2,1)S(1)}, bf16[100,1024]{1,0:T(8,128)(2,1)}, u32[]{:S(2)}) copy-start(bf16[100,1024]{1,0:T(8,128)(2,1)} %w_out.3) | copy-start | bytes 614404
  17.2 9.9 %copy-start.1 = (f32[512]{0:T(512)S(1)}, f32[512]{0:T(512)}, u32[]{:S(2)}) copy-start(f32[512]{0:T(512)} %param.12) | copy-start | bytes 6148
  17.2 9.9 %slice-start = ((f32[100,512]{1,0:T(8,128)}), f32[100,256]{1,0:T(8,128)S(1)}, s32[]{:S(2)}) async-start(f32[100,512]{1,0:T(8,128)} %targets.1), calls=%async_computation.1 | async-start | bytes 212992 | tf_op jit(solution)/shard_map/slice | solution.py:181
  17.2 19.2 %copy-start = (f32[100,512]{1,0:T(8,128)S(1)}, f32[100,512]{1,0:T(8,128)}, u32[]{:S(2)}) copy-start(f32[100,512]{1,0:T(8,128)} %targets.1) | copy-start | bytes 614404
  17.2 19.1 %copy-start.3 = (bf16[1024,1024]{1,0:T(8,128)(2,1)S(1)}, bf16[1024,1024]{1,0:T(8,128)(2,1)}, u32[]{:S(2)}) copy-start(bf16[1024,1024]{1,0:T(8,128)(2,1)} %w_in.5) | copy-start | bytes 6291460
  20.0 16.4 %all-to-all-start = ((bf16[8,100,512]{2,1,0:T(8,128)(2,1)}), bf16[8,100,512]{2,1,0:T(8,128)(2,1)S(1)}, u32[]{:S(2)}, u32[]{:S(2)}) async-start(bf16[8,100,512]{2,1,0:T(8,128)(2,1)} %get-tuple-element.15), calls=%async_computation | async-start | bytes 1703936 | tf_op jit(solution)/shard_map/all_to_all | solution.py:201
  27.1 8.1 %collective-permute-start.1 = (f32[101,256]{1,0:T(8,128)S(1)}, f32[101,256]{1,0:T(8,128)S(1)}, u32[]{:S(2)}, u32[]{:S(2)}) collective-permute-start(f32[101,256]{1,0:T(8,128)S(1)} %pad_maximum_fusion.1), channel_id=1, source_target_pairs={{0,1},{1,2},{2,3},{3,4},{4,5},{5,6},{6,7},{7,8},{8,9},{9,10},{10,1... | collective-permute-start | bytes 310280 | tf_op jit(solution)/shard_map/ppermute | solution.py:18
  39.6 7.4 %collective-permute-start.2 = (bf16[64,1024]{1,0:T(8,128)(2,1)S(1)}, bf16[64,1024]{1,0:T(8,128)(2,1)S(1)}, u32[]{:S(2)}, u32[]{:S(2)}) collective-permute-start(bf16[64,1024]{1,0:T(8,128)(2,1)S(1)} %get-tuple-element.18), channel_id=1, source_target_pairs={{0,63},{1,0},{2,1},{3,2},{4,3},{5,4},{6,5},{7,6},{8,7},{9,8},{10,9... | collective-permute-start | bytes 393224 | tf_op jit(solution)/shard_map/ppermute | solution.py:18

commit v4 on v3

v4 whole, which is shorter than its diff:
```python
import jax
import jax.numpy as jnp
from jax import lax
from jax.experimental import pallas as pl
from jax.experimental.pallas import tpu as pltpu
from jax.sharding import PartitionSpec as P

smooth = 0.0025
bf16 = jnp.bfloat16
f32 = jnp.float32
STEP = 256
LIMITS = (16, 16, 16)
SLOTS = 4


def shifted(block, axis, by):
    size = lax.axis_size(axis)
    return lax.ppermute(block, axis, [(i, (i + by) % size) for i in range(size)])


def slope(diff):
    return diff * lax.rsqrt(diff * diff + smooth)


def product(left, right, over):
    return lax.dot_general(left, right, (over, ((), ())), preferred_element_type=f32)


def adjacent(span, edges):
    slots, half = SLOTS, edges.shape[1]
    row = lax.broadcasted_iota(jnp.int32, (span, half), 0)
    total = jnp.zeros((span, half), f32)
    for k in range(slots):
        place = edges[k : k + 1].astype(jnp.int32)
        total = total + jnp.where(row == place, edges[slots + k : slots + k + 1], 0.0)
    return total.astype(bf16)


def halves(part):
    top = part.astype(bf16)
    return top, (part - top.astype(f32)).astype(bf16)


def pack_kernel(latent, place, coef, message):
    rows, (slots, points) = latent.shape[0], place.shape
    message[:rows] = latent[...]
    blank = jnp.zeros((16 - 2 * slots, points), f32)
    tail = jnp.concatenate([place[...], coef[...], blank], axis=0)
    message[rows:, :points] = tail.astype(bf16)
    message[rows:, points:] = jnp.zeros((16, message.shape[1] - points), bf16)


def goal_kernel(targets, area, message):
    count, half = targets.shape[0], message.shape[1]
    message[:count] = targets[:, half:]
    message[count : count + 1] = area[:, half:]


def own_kernel(message, w_in, own_top, own_rest, own_edges):
    rows, channels = own_top.shape
    span, half = own_edges.shape
    own_edges[...] = adjacent(span, message[rows:, :half].astype(f32))
    for c in range(0, channels, STEP):
        cut = slice(c, c + STEP)
        part = product(message[:rows], w_in[:, cut], ((1,), (0,)))
        own_top[:, cut], own_rest[:, cut] = halves(part)


def forward_kernel(
    message, own_top, own_rest, own_edges, w_in, w_out, copies, field, gate, edges, mixed, hidden
):
    rows, channels = own_top.shape
    span, half = own_edges.shape
    edges[:, :half] = adjacent(span, message[rows:, half : 2 * half].astype(f32))
    edges[:, half:] = own_edges[...]
    both = edges[...]
    twice = jnp.concatenate([both, both], axis=0)
    for c in range(0, channels, STEP):
        cut = slice(c, c + STEP)
        part = product(message[:rows], w_in[:, cut], ((1,), (0,)))
        mixed[:rows, cut], mixed[span : span + rows, cut] = halves(part)
    mixed[rows:span] = own_top[...]
    mixed[span + rows :] = own_rest[...]
    for c in range(0, channels, STEP):
        cut = slice(c, c + STEP)
        pre = product(mixed[:, cut], twice, ((0,), (0,)))
        sigma = 1.0 / (1.0 + jnp.exp(-pre))
        act = pre * sigma
        hidden[cut] = act.astype(bf16)
        gate[cut] = sigma + act * (1.0 - sigma)
    out = product(w_out[...], hidden[...], ((1,), (0,)))
    field[...] = out
    rounded = out.astype(bf16)
    for m in range(copies.shape[0]):
        copies[m] = rounded


def backward_kernel(
    every, moved, targets, area, w_out, w_in, field, gate, edges, out, rim, joined
):
    members, count, points = every.shape
    half = points // 2
    rows, channels = out.shape
    me = lax.axis_index("member")
    own = every[me].astype(f32)
    total = jnp.zeros((count, points), f32)
    for m in range(members):
        total = total + slope(own - every[m].astype(f32))
    goal = jnp.concatenate([moved[:count], targets[:, :half]], axis=1)
    scale = jnp.concatenate([moved[count : count + 1], area[:, :half]], axis=1)
    pull = slope(field[...] - goal) - total * (1.0 / (members - 1))
    grad_field = (scale * pull).astype(bf16)
    for c in range(0, channels, STEP):
        cut = slice(c, c + STEP)
        grad_hidden = product(w_out[:, cut], grad_field, ((0,), (0,)))
        grad_pre = (grad_hidden * gate[cut]).astype(bf16)
        joined[:, cut] = product(edges[...], grad_pre, ((1,), (1,))).astype(bf16)
    for c in range(0, channels, STEP):
        cut = slice(c, c + STEP)
        part = product(joined[...], w_in[cut], ((1,), (1,)))
        rim[:, cut] = part[:rows].astype(bf16)
        out[:, cut] = part[rows:]


HERE = pl.BlockSpec(memory_space=pltpu.VMEM)


def call(kernel, limit, ins, outs, scratch):
    return pl.pallas_call(
        kernel,
        out_shape=[jax.ShapeDtypeStruct(dims, kind) for _, dims, kind in outs],
        in_specs=[spec for spec, _ in ins],
        out_specs=[spec for spec, _, _ in outs],
        scratch_shapes=[pltpu.VMEM(dims, kind) for dims, kind in scratch],
        compiler_params=pltpu.CompilerParams(vmem_limit_bytes=limit << 20),
        cost_estimate=pl.CostEstimate(flops=10**10, bytes_accessed=4 << 20, transcendentals=0),
    )(*[operand for _, operand in ins])


def per_device(latent, neighbours, live, edge_weight, area, targets, w_in, w_out):
    rows, channels = latent.shape[1:]
    slots, points = neighbours.shape
    fields = targets.shape[0]
    half = points // 2
    mesh_rows = rows * lax.axis_size("space")
    members = lax.axis_size("member")
    span = 2 * rows

    column = lax.broadcasted_iota(jnp.int32, (slots, points), 1)
    first = (lax.axis_index("space") - (column < half)) * rows
    place = jnp.bitwise_and(neighbours - first, mesh_rows - 1).astype(f32)
    coef = edge_weight.astype(f32) * live.astype(f32)
    edge = 4.0 * place + coef
    place = jnp.floor(0.25 * edge)
    coef = edge - 4.0 * place
    (message,) = call(
        pack_kernel,
        LIMITS[0],
        [(HERE, x) for x in (latent[0], place, coef)],
        [(HERE, (rows + 16, channels), bf16)],
        [],
    )
    received = shifted(message, "space", 1)
    own_top, own_rest, own_edges = call(
        own_kernel,
        LIMITS[0],
        [(HERE, message), (HERE, w_in)],
        [(HERE, (rows, channels), bf16), (HERE, (rows, channels), bf16), (HERE, (span, half), bf16)],
        [],
    )
    own_edges, targets, area = lax.optimization_barrier((own_edges, targets, area[None]))
    (goals,) = call(
        goal_kernel, LIMITS[0], [(HERE, targets), (HERE, area)], [(HERE, (fields + 4, half), f32)], []
    )
    moved = shifted(goals, "space", 1)
    copies, field, gate, edges = call(
        forward_kernel,
        LIMITS[1],
        [(HERE, x) for x in (received, own_top, own_rest, own_edges, w_in, w_out)],
        [
            (HERE, (members, fields, points), bf16),
            (HERE, (fields, points), f32),
            (HERE, (channels, points), f32),
            (HERE, (span, points), bf16),
        ],
        [((2 * span, channels), bf16), ((channels, points), bf16)],
    )
    copies, moved = lax.optimization_barrier((copies, moved))
    every = lax.all_to_all(copies, "member", 0, 0, tiled=True)
    inner, rim = call(
        backward_kernel,
        LIMITS[2],
        [(HERE, x) for x in (every, moved, targets, area, w_out, w_in, field, gate, edges)],
        [(HERE, (rows, channels), f32), (HERE, (rows, channels), bf16)],
        [((span, channels), bf16)],
    )
    after = shifted(rim, "space", -1)
    return (inner + after.astype(f32)).astype(bf16)[None]


def solution(mesh):
    return jax.shard_map(
        per_device,
        mesh=mesh,
        in_specs=(
            P("member", "space", None),
            P(None, "space"),
            P(None, "space"),
            P(None, "space"),
            P("space"),
            P(None, "space"),
            P(),
            P(),
        ),
        out_specs=P("member", "space", None),
        check_vma=False,
    )
```

time: 48 us -> 44.6 us (0.929)
  the two profiles are of different devices: /device:TPU:4 before, /device:TPU:1 now
where the time goes in v4:
time: 44.6 us; the launch traced here: 44.3 us
  starting transfers between devices  19.6 us (44%)
  blocking collectives  13.8 us (31%)
  waiting for transfers between devices  4.41 us (10%)
  Pallas kernels  4.09 us (9%)
  other arithmetic  1.43 us (3%)
  local copies, waits for them, and re-layouts  0.92 us (2%)
    ppermute x3, starting transfers between devices, shifted(): lax.ppermute(block, axis, [(i, (i + by) % size) for i in range(size)])  19.6 us
    all_to_all x1, blocking collectives, per_device(): every = lax.all_to_all(copies, 'member', 0, 0, tiled=True)  13.8 us
    ppermute x3, waiting for transfers between devices, shifted(): lax.ppermute(block, axis, [(i, (i + by) % size) for i in range(size)])  4.41 us
    pallas_call x5, Pallas kernels, call(): pl.pallas_call(kernel, out_shape=[jax.ShapeDtypeStruct(dims, kind) for _,...  4.09 us
    unnamed x10, local copies, waits for them, and re-layouts  0.92 us
  transfers between devices with their start and end apart: 3, of which 3 were waited for; matrix products, arithmetic and copies ran while one was open for 0% of the time, Pallas kernels for 5%

profile of v4, /device:TPU:1, one launch (start us, length us, event | category | flops | bytes accessed | tf_op | source)
XLA Modules:
  0.0 44.3 jit_solution(6617649553036431330)
XLA Ops:
  0.0 0.7 %multiply_subtract_fusion = (f32[4,512]{1,0:T(4,128)S(1)}, f32[4,512]{1,0:T(4,128)S(1)}) fusion(s32[4,512]{1,0:T(4,128)} %param.10, bf16[4,512]{1,0:T(4,128)(2,1)} %param.11, s32[4,512]{1,0:T(4,128)} %param.9, s32[512]{0:T(512)S(1)} %subtract_multiply_fusion), kind=kLoop, calls=%fused_computation.2 | loop fusion | flops 24576 | bytes 38912 | tf_op jit(solution)/shard_map/sub | solution.py:155
  0.8 0.0 copy-start.3
  0.8 0.9 %copy-done.3 = bf16[1,64,1024]{2,1,0:T(8,128)(2,1)S(1)} copy-done((bf16[1,64,1024]{2,1,0:T(8,128)(2,1)S(1)}, bf16[1,64,1024]{2,1,0:T(8,128)(2,1)}, u32[]{:S(2)}) %copy-start.3) | copy-done | bytes 131096
  1.7 0.0 copy-start
  1.7 0.0 copy-start.2
  1.7 0.0 copy-start.4
  1.7 4.7 %collective-permute-start = (bf16[80,1024]{1,0:T(8,128)(2,1)S(1)}, bf16[80,1024]{1,0:T(8,128)(2,1)S(1)}, u32[]{:S(2)}, u32[]{:S(2)}) collective-permute-start(bf16[80,1024]{1,0:T(8,128)(2,1)S(1)} %shard_map.82.message), channel_id=1, source_target_pairs={{0,1},{1,2},{2,3},{3,4},{4,5},{5,6},{6,7},{7,8},{8,9},{9,10},{10,1... | collective-permute-start | bytes 491528 | tf_op jit(solution)/shard_map/ppermute | solution.py:18
  6.4 0.0 copy-done
  6.4 0.6 %shard_map.83 = (bf16[64,1024]{1,0:T(8,128)(2,1)S(1)}, bf16[64,1024]{1,0:T(8,128)(2,1)S(1)}, bf16[128,256]{1,0:T(8,128)(2,1)S(1)}) custom-call(bf16[80,1024]{1,0:T(8,128)(2,1)S(1)} %shard_map.82.message, bf16[1024,1024]{1,0:T(8,128)(2,1)S(1)} %copy-done), custom_call_target="tpu_custom_call" | custom-call | flops 10000000000 | bytes 4194304 | tf_op jit(solution)/shard_map/pallas_call | solution.py:129
  7.0 0.0 copy-done.2
  7.0 0.0 copy-done.4
  7.0 0.0 copy-start.1
  7.1 2.1 %collective-permute-start.1 = (f32[104,256]{1,0:T(8,128)S(1)}, f32[104,256]{1,0:T(8,128)S(1)}, u32[]{:S(2)}, u32[]{:S(2)}) collective-permute-start(f32[104,256]{1,0:T(8,128)S(1)} %shard_map.85), channel_id=1, source_target_pairs={{0,1},{1,2},{2,3},{3,4},{4,5},{5,6},{6,7},{7,8},{8,9},{9,10},{10,1... | collective-permute-start | bytes 319496 | tf_op jit(solution)/shard_map/ppermute | solution.py:18
  9.1 2.4 %collective-permute-done.message = bf16[80,1024]{1,0:T(8,128)(2,1)S(1)} collective-permute-done((bf16[80,1024]{1,0:T(8,128)(2,1)S(1)}, bf16[80,1024]{1,0:T(8,128)(2,1)S(1)}, u32[]{:S(2)}, u32[]{:S(2)}) %collective-permute-start) | collective-permute-done | bytes 163872 | tf_op jit(solution)/shard_map/ppermute | solution.py:18
  11.5 0.0 copy-done.1
  11.5 1.5 %shard_map.84 = (bf16[8,100,512]{2,1,0:T(8,128)(2,1)S(1)}, f32[100,512]{1,0:T(8,128)S(1)}, f32[1024,512]{1,0:T(8,128)S(1)}, bf16[128,512]{1,0:T(8,128)(2,1)S(1)}) custom-call(bf16[80,1024]{1,0:T(8,128)(2,1)S(1)} %collective-permute-done.message, bf16[64,1024]{1,0:T(8,128)(2,1)S(1)} %get-tuple-element.19.own_top, ...), custom_call_target="tpu_custom_call" | custom-call | flops 10000000000 | bytes 4194304 | tf_op jit(solution)/shard_map/pallas_call | solution.py:129
  13.0 1.1 %collective-permute-done.1.moved = f32[104,256]{1,0:T(8,128)S(1)} collective-permute-done((f32[104,256]{1,0:T(8,128)S(1)}, f32[104,256]{1,0:T(8,128)S(1)}, u32[]{:S(2)}, u32[]{:S(2)}) %collective-permute-start.1) | collective-permute-done | bytes 106528 | tf_op jit(solution)/shard_map/ppermute | solution.py:18
  14.1 13.8 %all_to_all.5.every = bf16[8,100,512]{2,1,0:T(8,128)(2,1)S(1)} all-to-all(bf16[8,100,512]{2,1,0:T(8,128)(2,1)S(1)} %get-tuple-element.26), channel_id=1, replica_groups=mesh['member'=8,'space'=64] {'member'}, dimensions={0} | all-to-all | bytes 1638400 | tf_op jit(solution)/shard_map/all_to_all | solution.py:189
  27.9 2.0 %shard_map.86 = (f32[64,1024]{1,0:T(8,128)S(1)}, bf16[64,1024]{1,0:T(8,128)(2,1)S(1)}) custom-call(bf16[8,100,512]{2,1,0:T(8,128)(2,1)S(1)} %all_to_all.5.every, f32[104,256]{1,0:T(8,128)S(1)} %collective-permute-done.1.moved, f32[100,512]{1,0:T(8,128)S(1)} %copy-done.2, f32[1,512]{1,0:T(1,128)S(1)} %bitcast.6, bf16[100,1024]{1,0:T(8,128)(2,1)S(1)} %copy-done.1, ...), custom_call_target="tpu_custom_call" | custom-call | flops 10000000000 | bytes 4194304 | tf_op jit(solution)/shard_map/pallas_call | solution.py:129
  29.9 12.8 %collective-permute-start.2 = (bf16[64,1024]{1,0:T(8,128)(2,1)S(1)}, bf16[64,1024]{1,0:T(8,128)(2,1)S(1)}, u32[]{:S(2)}, u32[]{:S(2)}) collective-permute-start(bf16[64,1024]{1,0:T(8,128)(2,1)S(1)} %get-tuple-element.32), channel_id=1, source_target_pairs={{0,63},{1,0},{2,1},{3,2},{4,3},{5,4},{6,5},{7,6},{8,7},{9,8},{10,9... | collective-permute-start | bytes 393224 | tf_op jit(solution)/shard_map/ppermute | solution.py:18
  42.7 1.0 %collective-permute-done.2 = bf16[64,1024]{1,0:T(8,128)(2,1)S(1)} collective-permute-done((bf16[64,1024]{1,0:T(8,128)(2,1)S(1)}, bf16[64,1024]{1,0:T(8,128)(2,1)S(1)}, u32[]{:S(2)}, u32[]{:S(2)}) %collective-permute-start.2) | collective-permute-done | bytes 131104 | tf_op jit(solution)/shard_map/ppermute | solution.py:18
  43.6 0.7 %fusion = bf16[1,64,1024]{2,1,0:T(8,128)(2,1)} fusion(f32[64,1024]{1,0:T(8,128)S(1)} %get-tuple-element.31, bf16[64,1024]{1,0:T(8,128)(2,1)S(1)} %collective-permute-done.2), kind=kLoop, calls=%fused_computation.1 | loop fusion | flops 196608 | bytes 524288 | tf_op jit(solution)/shard_map/broadcast_in_dim | solution.py:198
  (3 shorter events, 0.0 us)
Async XLA Ops:
  0.8 0.9 %copy-start.3 = (bf16[1,64,1024]{2,1,0:T(8,128)(2,1)S(1)}, bf16[1,64,1024]{2,1,0:T(8,128)(2,1)}, u32[]{:S(2)}) copy-start(bf16[1,64,1024]{2,1,0:T(8,128)(2,1)} %param.8) | copy-start | bytes 393220
  1.7 4.8 %copy-start = (bf16[1024,1024]{1,0:T(8,128)(2,1)S(1)}, bf16[1024,1024]{1,0:T(8,128)(2,1)}, u32[]{:S(2)}) copy-start(bf16[1024,1024]{1,0:T(8,128)(2,1)} %w_in.5) | copy-start | bytes 6291460
  1.7 5.4 %copy-start.2 = (f32[100,512]{1,0:T(8,128)S(1)}, f32[100,512]{1,0:T(8,128)}, u32[]{:S(2)}) copy-start(f32[100,512]{1,0:T(8,128)} %targets.1) | copy-start | bytes 614404
  1.7 5.3 %copy-start.4 = (f32[512]{0:T(512)S(1)}, f32[512]{0:T(512)}, u32[]{:S(2)}) copy-start(f32[512]{0:T(512)} %param.12) | copy-start | bytes 6148
  1.7 9.8 %collective-permute-start = (bf16[80,1024]{1,0:T(8,128)(2,1)S(1)}, bf16[80,1024]{1,0:T(8,128)(2,1)S(1)}, u32[]{:S(2)}, u32[]{:S(2)}) collective-permute-start(bf16[80,1024]{1,0:T(8,128)(2,1)S(1)} %shard_map.82.message), channel_id=1, source_target_pairs={{0,1},{1,2},{2,3},{3,4},{4,5},{5,6},{6,7},{7,8},{8,9},{9,10},{10,1... | collective-permute-start | bytes 491528 | tf_op jit(solution)/shard_map/ppermute | solution.py:18
  7.0 4.5 %copy-start.1 = (bf16[100,1024]{1,0:T(8,128)(2,1)S(1)}, bf16[100,1024]{1,0:T(8,128)(2,1)}, u32[]{:S(2)}) copy-start(bf16[100,1024]{1,0:T(8,128)(2,1)} %w_out.3) | copy-start | bytes 614404
  7.1 7.0 %collective-permute-start.1 = (f32[104,256]{1,0:T(8,128)S(1)}, f32[104,256]{1,0:T(8,128)S(1)}, u32[]{:S(2)}, u32[]{:S(2)}) collective-permute-start(f32[104,256]{1,0:T(8,128)S(1)} %shard_map.85), channel_id=1, source_target_pairs={{0,1},{1,2},{2,3},{3,4},{4,5},{5,6},{6,7},{7,8},{8,9},{9,10},{10,1... | collective-permute-start | bytes 319496 | tf_op jit(solution)/shard_map/ppermute | solution.py:18
  29.9 13.8 %collective-permute-start.2 = (bf16[64,1024]{1,0:T(8,128)(2,1)S(1)}, bf16[64,1024]{1,0:T(8,128)(2,1)S(1)}, u32[]{:S(2)}, u32[]{:S(2)}) collective-permute-start(bf16[64,1024]{1,0:T(8,128)(2,1)S(1)} %get-tuple-element.32), channel_id=1, source_target_pairs={{0,63},{1,0},{2,1},{3,2},{4,3},{5,4},{6,5},{7,6},{8,7},{9,8},{10,9... | collective-permute-start | bytes 393224 | tf_op jit(solution)/shard_map/ppermute | solution.py:18

commit v5 on v4

--- a/solution.py
+++ b/solution.py
@@ -41,25 +41,19 @@
     return top, (part - top.astype(f32)).astype(bf16)
 
 
-def pack_kernel(latent, place, coef, message):
-    rows, (slots, points) = latent.shape[0], place.shape
-    message[:rows] = latent[...]
-    blank = jnp.zeros((16 - 2 * slots, points), f32)
-    tail = jnp.concatenate([place[...], coef[...], blank], axis=0)
-    message[rows:, :points] = tail.astype(bf16)
-    message[rows:, points:] = jnp.zeros((16, message.shape[1] - points), bf16)
-
-
 def goal_kernel(targets, area, message):
     count, half = targets.shape[0], message.shape[1]
     message[:count] = targets[:, half:]
     message[count : count + 1] = area[:, half:]
 
 
-def own_kernel(message, w_in, own_top, own_rest, own_edges):
+def edge_kernel(message, own_edges):
+    span, half = own_edges.shape
+    own_edges[...] = adjacent(span, message[span // 2 :, :half].astype(f32))
+
+
+def own_kernel(message, w_in, own_top, own_rest):
     rows, channels = own_top.shape
-    span, half = own_edges.shape
-    own_edges[...] = adjacent(span, message[rows:, :half].astype(f32))
     for c in range(0, channels, STEP):
         cut = slice(c, c + STEP)
         part = product(message[:rows], w_in[:, cut], ((1,), (0,)))
@@ -146,33 +140,32 @@
     members = lax.axis_size("member")
     span = 2 * rows
 
-    column = lax.broadcasted_iota(jnp.int32, (slots, points), 1)
+    tall, blank = rows + 16, channels - points
+    row = lax.broadcasted_iota(jnp.int32, (tall, channels), 0)
+    column = lax.broadcasted_iota(jnp.int32, (tall, channels), 1)
+
+    def placed(block, start):
+        return jnp.pad(block, ((start, tall - start - block.shape[0]), (0, channels - block.shape[1])))
+
     first = (lax.axis_index("space") - (column < half)) * rows
-    place = jnp.bitwise_and(neighbours - first, mesh_rows - 1).astype(f32)
-    coef = edge_weight.astype(f32) * live.astype(f32)
-    edge = 4.0 * place + coef
-    place = jnp.floor(0.25 * edge)
-    coef = edge - 4.0 * place
-    (message,) = call(
-        pack_kernel,
-        LIMITS[0],
-        [(HERE, x) for x in (latent[0], place, coef)],
-        [(HERE, (rows + 16, channels), bf16)],
-        [],
-    )
+    place = jnp.bitwise_and(placed(neighbours, rows) - first, mesh_rows - 1).astype(bf16)
+    coef = placed(edge_weight, rows + slots).astype(f32) * placed(live, rows + slots).astype(f32)
+    edge = jnp.where(row < rows + slots, place, coef.astype(bf16))
+    message = jnp.where(row < rows, placed(latent[0], 0), edge)
     received = shifted(message, "space", 1)
-    own_top, own_rest, own_edges = call(
+    (own_edges,) = call(edge_kernel, LIMITS[0], [(HERE, message)], [(HERE, (span, half), bf16)], [])
+    own_edges, targets, area = lax.optimization_barrier((own_edges, targets, area[None]))
+    (goals,) = call(
+        goal_kernel, LIMITS[0], [(HERE, targets), (HERE, area)], [(HERE, (fields + 4, half), f32)], []
+    )
+    moved = shifted(goals, "space", 1)
+    own_top, own_rest = call(
         own_kernel,
         LIMITS[0],
         [(HERE, message), (HERE, w_in)],
-        [(HERE, (rows, channels), bf16), (HERE, (rows, channels), bf16), (HERE, (span, half), bf16)],
+        [(HERE, (rows, channels), bf16), (HERE, (rows, channels), bf16)],
         [],
     )
-    own_edges, targets, area = lax.optimization_barrier((own_edges, targets, area[None]))
-    (goals,) = call(
-        goal_kernel, LIMITS[0], [(HERE, targets), (HERE, area)], [(HERE, (fields + 4, half), f32)], []
-    )
-    moved = shifted(goals, "space", 1)
     copies, field, gate, edges = call(
         forward_kernel,
         LIMITS[1],

time: 44.6 us -> 43.4 us (0.973)
  local copies, waits for them, and re-layouts: 0.92 us -> 0.03 us
  waiting for transfers between devices: 4.41 us -> 3.91 us
    select_n x0 -> x1, other arithmetic: none -> 1.07 us  [per_device(): message = jnp.where(row < rows, placed(latent[0], 0), edge)]
    unnamed x10 -> x8, local copies, waits for them, and re-layouts: 0.92 us -> 0.03 us
    sub x1 -> x0, other arithmetic: 0.74 us -> none  [per_device(): coef = edge - 4.0 * place]
    ppermute x3, waiting for transfers between devices: 4.41 us -> 3.91 us  [shifted(): lax.ppermute(block, axis, [(i, (i + by) % size) for i in range(size)])]
where the time goes in v5:
time: 43.4 us; the launch traced here: 43.2 us
  starting transfers between devices  19.2 us (44%)
  blocking collectives  14.2 us (33%)
  Pallas kernels  4.05 us (9%)
  waiting for transfers between devices  3.91 us (9%)
  other arithmetic  1.76 us (4%)
    ppermute x3, starting transfers between devices, shifted(): lax.ppermute(block, axis, [(i, (i + by) % size) for i in range(size)])  19.2 us
    all_to_all x1, blocking collectives, per_device(): every = lax.all_to_all(copies, 'member', 0, 0, tiled=True)  14.2 us
    pallas_call x5, Pallas kernels, call(): pl.pallas_call(kernel, out_shape=[jax.ShapeDtypeStruct(dims, kind) for _,...  4.05 us
    ppermute x3, waiting for transfers between devices, shifted(): lax.ppermute(block, axis, [(i, (i + by) % size) for i in range(size)])  3.91 us
    select_n x1, other arithmetic, per_device(): message = jnp.where(row < rows, placed(latent[0], 0), edge)  1.07 us
  transfers between devices with their start and end apart: 3, of which 3 were waited for; matrix products, arithmetic and copies ran while one was open for 0% of the time, Pallas kernels for 5%

profile of v5, /device:TPU:1, one launch (start us, length us, event | category | flops | bytes accessed | tf_op | source)
XLA Modules:
  0.0 43.2 jit_solution(1167554863514946427)
XLA Ops:
  0.0 1.1 %fusion.1.message = bf16[80,1024]{1,0:T(8,128)(2,1)S(1)} fusion(s32[4,512]{1,0:T(4,128)} %param.9, s32[4,512]{1,0:T(4,128)} %param.10, bf16[4,512]{1,0:T(4,128)(2,1)} %param.11, s32[1024]{0:T(1024)S(1)} %subtract_multiply_fusion, bf16[64,1024]{1,0:T(8,128)(2,1)} %bitcast.6, pred[80]{0:T(512)(128)(4,1)S(1)} %get-tuple-element.31, ...), kind=kLoop, calls=%fused_computation.4 | loop fusion | flops 737280 | bytes 319648 | tf_op jit(solution)/shard_map/jit(_where)/select_n | solution.py:154
  1.1 0.0 copy-start.2
  1.1 0.0 copy-start.3
  1.1 4.7 %collective-permute-start = (bf16[80,1024]{1,0:T(8,128)(2,1)S(1)}, bf16[80,1024]{1,0:T(8,128)(2,1)S(1)}, u32[]{:S(2)}, u32[]{:S(2)}) collective-permute-start(bf16[80,1024]{1,0:T(8,128)(2,1)S(1)} %fusion.1.message), channel_id=1, source_target_pairs={{0,1},{1,2},{2,3},{3,4},{4,5},{5,6},{6,7},{7,8},{8,9},{9,10},{10,1... | collective-permute-start | bytes 491528 | tf_op jit(solution)/shard_map/ppermute | solution.py:18
  5.8 0.1 shard_map.83.own_edges
  5.9 0.0 copy-done.2
  5.9 0.0 copy-done.3
  5.9 0.0 copy-start
  6.0 0.0 copy-start.1
  6.0 2.1 %collective-permute-start.1 = (f32[104,256]{1,0:T(8,128)S(1)}, f32[104,256]{1,0:T(8,128)S(1)}, u32[]{:S(2)}, u32[]{:S(2)}) collective-permute-start(f32[104,256]{1,0:T(8,128)S(1)} %shard_map.85), channel_id=1, source_target_pairs={{0,1},{1,2},{2,3},{3,4},{4,5},{5,6},{6,7},{7,8},{8,9},{9,10},{10,1... | collective-permute-start | bytes 319496 | tf_op jit(solution)/shard_map/ppermute | solution.py:18
  8.0 0.0 copy-done
  8.0 0.5 %shard_map.82 = (bf16[64,1024]{1,0:T(8,128)(2,1)S(1)}, bf16[64,1024]{1,0:T(8,128)(2,1)S(1)}) custom-call(bf16[80,1024]{1,0:T(8,128)(2,1)S(1)} %fusion.1.message, bf16[1024,1024]{1,0:T(8,128)(2,1)S(1)} %copy-done), custom_call_target="tpu_custom_call" | custom-call | flops 10000000000 | bytes 4194304 | tf_op jit(solution)/shard_map/pallas_call | solution.py:123
  8.5 2.4 %collective-permute-done.message = bf16[80,1024]{1,0:T(8,128)(2,1)S(1)} collective-permute-done((bf16[80,1024]{1,0:T(8,128)(2,1)S(1)}, bf16[80,1024]{1,0:T(8,128)(2,1)S(1)}, u32[]{:S(2)}, u32[]{:S(2)}) %collective-permute-start) | collective-permute-done | bytes 163872 | tf_op jit(solution)/shard_map/ppermute | solution.py:18
  10.9 0.0 copy-done.1
  10.9 1.5 %shard_map.84 = (bf16[8,100,512]{2,1,0:T(8,128)(2,1)S(1)}, f32[100,512]{1,0:T(8,128)S(1)}, f32[1024,512]{1,0:T(8,128)S(1)}, bf16[128,512]{1,0:T(8,128)(2,1)S(1)}) custom-call(bf16[80,1024]{1,0:T(8,128)(2,1)S(1)} %collective-permute-done.message, bf16[64,1024]{1,0:T(8,128)(2,1)S(1)} %get-tuple-element.18.own_top, ...), custom_call_target="tpu_custom_call" | custom-call | flops 10000000000 | bytes 4194304 | tf_op jit(solution)/shard_map/pallas_call | solution.py:123
  12.4 0.6 %collective-permute-done.1.moved = f32[104,256]{1,0:T(8,128)S(1)} collective-permute-done((f32[104,256]{1,0:T(8,128)S(1)}, f32[104,256]{1,0:T(8,128)S(1)}, u32[]{:S(2)}, u32[]{:S(2)}) %collective-permute-start.1) | collective-permute-done | bytes 106528 | tf_op jit(solution)/shard_map/ppermute | solution.py:18
  13.0 14.2 %all_to_all.5.every = bf16[8,100,512]{2,1,0:T(8,128)(2,1)S(1)} all-to-all(bf16[8,100,512]{2,1,0:T(8,128)(2,1)S(1)} %get-tuple-element.24), channel_id=1, replica_groups=mesh['member'=8,'space'=64] {'member'}, dimensions={0} | all-to-all | bytes 1638400 | tf_op jit(solution)/shard_map/all_to_all | solution.py:182
  27.2 2.0 %shard_map.86 = (f32[64,1024]{1,0:T(8,128)S(1)}, bf16[64,1024]{1,0:T(8,128)(2,1)S(1)}) custom-call(bf16[8,100,512]{2,1,0:T(8,128)(2,1)S(1)} %all_to_all.5.every, f32[104,256]{1,0:T(8,128)S(1)} %collective-permute-done.1.moved, f32[100,512]{1,0:T(8,128)S(1)} %copy-done.2, f32[1,512]{1,0:T(1,128)S(1)} %bitcast.5, bf16[100,1024]{1,0:T(8,128)(2,1)S(1)} %copy-done.1, ...), custom_call_target="tpu_custom_call" | custom-call | flops 10000000000 | bytes 4194304 | tf_op jit(solution)/shard_map/pallas_call | solution.py:123
  29.1 12.4 %collective-permute-start.2 = (bf16[64,1024]{1,0:T(8,128)(2,1)S(1)}, bf16[64,1024]{1,0:T(8,128)(2,1)S(1)}, u32[]{:S(2)}, u32[]{:S(2)}) collective-permute-start(bf16[64,1024]{1,0:T(8,128)(2,1)S(1)} %get-tuple-element.30), channel_id=1, source_target_pairs={{0,63},{1,0},{2,1},{3,2},{4,3},{5,4},{6,5},{7,6},{8,7},{9,8},{10,9... | collective-permute-start | bytes 393224 | tf_op jit(solution)/shard_map/ppermute | solution.py:18
  41.5 1.0 %collective-permute-done.2 = bf16[64,1024]{1,0:T(8,128)(2,1)S(1)} collective-permute-done((bf16[64,1024]{1,0:T(8,128)(2,1)S(1)}, bf16[64,1024]{1,0:T(8,128)(2,1)S(1)}, u32[]{:S(2)}, u32[]{:S(2)}) %collective-permute-start.2) | collective-permute-done | bytes 131104 | tf_op jit(solution)/shard_map/ppermute | solution.py:18
  42.5 0.7 %fusion.2 = bf16[1,64,1024]{2,1,0:T(8,128)(2,1)} fusion(f32[64,1024]{1,0:T(8,128)S(1)} %get-tuple-element.29, bf16[64,1024]{1,0:T(8,128)(2,1)S(1)} %collective-permute-done.2), kind=kLoop, calls=%fused_computation.5 | loop fusion | flops 196608 | bytes 524288 | tf_op jit(solution)/shard_map/broadcast_in_dim | solution.py:191
  (3 shorter events, 0.0 us)
Async XLA Ops:
  1.1 4.8 %copy-start.2 = (f32[100,512]{1,0:T(8,128)S(1)}, f32[100,512]{1,0:T(8,128)}, u32[]{:S(2)}) copy-start(f32[100,512]{1,0:T(8,128)} %targets.1) | copy-start | bytes 614404
  1.1 4.8 %copy-start.3 = (f32[512]{0:T(512)S(1)}, f32[512]{0:T(512)}, u32[]{:S(2)}) copy-start(f32[512]{0:T(512)} %param.12) | copy-start | bytes 6148
  1.1 9.8 %collective-permute-start = (bf16[80,1024]{1,0:T(8,128)(2,1)S(1)}, bf16[80,1024]{1,0:T(8,128)(2,1)S(1)}, u32[]{:S(2)}, u32[]{:S(2)}) collective-permute-start(bf16[80,1024]{1,0:T(8,128)(2,1)S(1)} %fusion.1.message), channel_id=1, source_target_pairs={{0,1},{1,2},{2,3},{3,4},{4,5},{5,6},{6,7},{7,8},{8,9},{9,10},{10,1... | collective-permute-start | bytes 491528 | tf_op jit(solution)/shard_map/ppermute | solution.py:18
  5.9 2.1 %copy-start = (bf16[1024,1024]{1,0:T(8,128)(2,1)S(1)}, bf16[1024,1024]{1,0:T(8,128)(2,1)}, u32[]{:S(2)}) copy-start(bf16[1024,1024]{1,0:T(8,128)(2,1)} %w_in.5) | copy-start | bytes 6291460
  6.0 5.0 %copy-start.1 = (bf16[100,1024]{1,0:T(8,128)(2,1)S(1)}, bf16[100,1024]{1,0:T(8,128)(2,1)}, u32[]{:S(2)}) copy-start(bf16[100,1024]{1,0:T(8,128)(2,1)} %w_out.3) | copy-start | bytes 614404
  6.0 7.0 %collective-permute-start.1 = (f32[104,256]{1,0:T(8,128)S(1)}, f32[104,256]{1,0:T(8,128)S(1)}, u32[]{:S(2)}, u32[]{:S(2)}) collective-permute-start(f32[104,256]{1,0:T(8,128)S(1)} %shard_map.85), channel_id=1, source_target_pairs={{0,1},{1,2},{2,3},{3,4},{4,5},{5,6},{6,7},{7,8},{8,9},{9,10},{10,1... | collective-permute-start | bytes 319496 | tf_op jit(solution)/shard_map/ppermute | solution.py:18
  29.1 13.4 %collective-permute-start.2 = (bf16[64,1024]{1,0:T(8,128)(2,1)S(1)}, bf16[64,1024]{1,0:T(8,128)(2,1)S(1)}, u32[]{:S(2)}, u32[]{:S(2)}) collective-permute-start(bf16[64,1024]{1,0:T(8,128)(2,1)S(1)} %get-tuple-element.30), channel_id=1, source_target_pairs={{0,63},{1,0},{2,1},{3,2},{4,3},{5,4},{6,5},{7,6},{8,7},{9,8},{10,9... | collective-permute-start | bytes 393224 | tf_op jit(solution)/shard_map/ppermute | solution.py:18

commit v6 on v5

--- a/solution.py
+++ b/solution.py
@@ -9,6 +9,7 @@
 bf16 = jnp.bfloat16
 f32 = jnp.float32
 STEP = 256
+LANES = 128
 LIMITS = (16, 16, 16)
 SLOTS = 4
 
@@ -47,17 +48,36 @@
     message[count : count + 1] = area[:, half:]
 
 
+def packed(block):
+    count, points = block.shape
+    whole = count // 16 * 16
+    cuts = [slice(j, j + LANES) for j in range(0, points, LANES)]
+    return jnp.concatenate([block[:whole, cut] for cut in cuts] + [block[whole:, cut] for cut in cuts], axis=0)
+
+
+def unpacked(block, count):
+    parts = block.shape[0] // count
+    whole = count // 16 * 16
+    left, base = count - whole, parts * whole
+    high = [block[j * whole : (j + 1) * whole] for j in range(parts)]
+    low = [block[base + j * left : base + (j + 1) * left] for j in range(parts)]
+    return jnp.concatenate([jnp.concatenate(high, axis=1), jnp.concatenate(low, axis=1)], axis=0)
+
+
 def edge_kernel(message, own_edges):
     span, half = own_edges.shape
     own_edges[...] = adjacent(span, message[span // 2 :, :half].astype(f32))
 
 
-def own_kernel(message, w_in, own_top, own_rest):
+def own_kernel(message, w_in, own_top, own_rest, turned):
     rows, channels = own_top.shape
     for c in range(0, channels, STEP):
         cut = slice(c, c + STEP)
         part = product(message[:rows], w_in[:, cut], ((1,), (0,)))
         own_top[:, cut], own_rest[:, cut] = halves(part)
+    for c in range(0, channels, STEP):
+        cut = slice(c, c + STEP)
+        turned[:, cut] = w_in[cut].T
 
 
 def forward_kernel(
@@ -84,22 +104,24 @@
         gate[cut] = sigma + act * (1.0 - sigma)
     out = product(w_out[...], hidden[...], ((1,), (0,)))
     field[...] = out
-    rounded = out.astype(bf16)
+    rounded = packed(out).astype(bf16)
     for m in range(copies.shape[0]):
         copies[m] = rounded
 
 
 def backward_kernel(
-    every, moved, targets, area, w_out, w_in, field, gate, edges, out, rim, joined
+    every, moved, targets, area, w_out, turned, field, gate, edges, out, rim, joined
 ):
-    members, count, points = every.shape
+    members = every.shape[0]
+    count, points = field.shape
     half = points // 2
     rows, channels = out.shape
     me = lax.axis_index("member")
     own = every[me].astype(f32)
-    total = jnp.zeros((count, points), f32)
+    total = jnp.zeros(own.shape, f32)
     for m in range(members):
         total = total + slope(own - every[m].astype(f32))
+    total = unpacked(total, count)
     goal = jnp.concatenate([moved[:count], targets[:, :half]], axis=1)
     scale = jnp.concatenate([moved[count : count + 1], area[:, :half]], axis=1)
     pull = slope(field[...] - goal) - total * (1.0 / (members - 1))
@@ -111,7 +133,7 @@
         joined[:, cut] = product(edges[...], grad_pre, ((1,), (1,))).astype(bf16)
     for c in range(0, channels, STEP):
         cut = slice(c, c + STEP)
-        part = product(joined[...], w_in[cut], ((1,), (1,)))
+        part = product(joined[...], turned[:, cut], ((1,), (0,)))
         rim[:, cut] = part[:rows].astype(bf16)
         out[:, cut] = part[rows:]
 
@@ -140,7 +162,7 @@
     members = lax.axis_size("member")
     span = 2 * rows
 
-    tall, blank = rows + 16, channels - points
+    tall = rows + 8
     row = lax.broadcasted_iota(jnp.int32, (tall, channels), 0)
     column = lax.broadcasted_iota(jnp.int32, (tall, channels), 1)
 
@@ -159,11 +181,15 @@
         goal_kernel, LIMITS[0], [(HERE, targets), (HERE, area)], [(HERE, (fields + 4, half), f32)], []
     )
     moved = shifted(goals, "space", 1)
-    own_top, own_rest = call(
+    own_top, own_rest, turned = call(
         own_kernel,
         LIMITS[0],
         [(HERE, message), (HERE, w_in)],
-        [(HERE, (rows, channels), bf16), (HERE, (rows, channels), bf16)],
+        [
+            (HERE, (rows, channels), bf16),
+            (HERE, (rows, channels), bf16),
+            (HERE, (channels, channels), bf16),
+        ],
         [],
     )
     copies, field, gate, edges = call(
@@ -171,7 +197,7 @@
         LIMITS[1],
         [(HERE, x) for x in (received, own_top, own_rest, own_edges, w_in, w_out)],
         [
-            (HERE, (members, fields, points), bf16),
+            (HERE, (members, fields * points // LANES, LANES), bf16),
             (HERE, (fields, points), f32),
             (HERE, (channels, points), f32),
             (HERE, (span, points), bf16),
@@ -183,7 +209,7 @@
     inner, rim = call(
         backward_kernel,
         LIMITS[2],
-        [(HERE, x) for x in (every, moved, targets, area, w_out, w_in, field, gate, edges)],
+        [(HERE, x) for x in (every, moved, targets, area, w_out, turned, field, gate, edges)],
         [(HERE, (rows, channels), f32), (HERE, (rows, channels), bf16)],
         [((span, channels), bf16)],
     )

time: 43.4 us -> 43 us (level)
  no operation moved by 1% of the time
where the time goes in v6:
time: 43 us; the launch traced here: 42.8 us
  starting transfers between devices  19 us (44%)
  blocking collectives  14.3 us (33%)
  Pallas kernels  3.96 us (9%)
  waiting for transfers between devices  3.69 us (9%)
  other arithmetic  1.76 us (4%)
    ppermute x3, starting transfers between devices, shifted(): lax.ppermute(block, axis, [(i, (i + by) % size) for i in range(size)])  19 us
    all_to_all x1, blocking collectives, per_device(): every = lax.all_to_all(copies, 'member', 0, 0, tiled=True)  14.3 us
    pallas_call x5, Pallas kernels, call(): pl.pallas_call(kernel, out_shape=[jax.ShapeDtypeStruct(dims, kind) for _,...  3.96 us
    ppermute x3, waiting for transfers between devices, shifted(): lax.ppermute(block, axis, [(i, (i + by) % size) for i in range(size)])  3.69 us
    select_n x1, other arithmetic, per_device(): message = jnp.where(row < rows, placed(latent[0], 0), edge)  1.06 us
  transfers between devices with their start and end apart: 3, of which 3 were waited for; matrix products, arithmetic and copies ran while one was open for 0% of the time, Pallas kernels for 5%

profile of v6, /device:TPU:1, one launch (start us, length us, event | category | flops | bytes accessed | tf_op | source)
XLA Modules:
  0.0 42.8 jit_solution(17153297615842831935)
XLA Ops:
  0.0 1.1 %fusion.1.message = bf16[72,1024]{1,0:T(8,128)(2,1)S(1)} fusion(s32[4,512]{1,0:T(4,128)} %param.9, s32[4,512]{1,0:T(4,128)} %param.10, bf16[4,512]{1,0:T(4,128)(2,1)} %param.11, s32[1024]{0:T(1024)S(1)} %subtract_multiply_fusion, bf16[64,1024]{1,0:T(8,128)(2,1)} %bitcast.6, pred[72]{0:T(512)(128)(4,1)S(1)} %get-tuple-element.33, ...), kind=kLoop, calls=%fused_computation.4 | loop fusion | flops 663552 | bytes 303248 | tf_op jit(solution)/shard_map/jit(_where)/select_n | solution.py:176
  1.1 0.0 copy-start.2
  1.1 0.0 copy-start.3
  1.1 4.7 %collective-permute-start = (bf16[72,1024]{1,0:T(8,128)(2,1)S(1)}, bf16[72,1024]{1,0:T(8,128)(2,1)S(1)}, u32[]{:S(2)}, u32[]{:S(2)}) collective-permute-start(bf16[72,1024]{1,0:T(8,128)(2,1)S(1)} %fusion.1.message), channel_id=1, source_target_pairs={{0,1},{1,2},{2,3},{3,4},{4,5},{5,6},{6,7},{7,8},{8,9},{9,10},{10,1... | collective-permute-start | bytes 442376 | tf_op jit(solution)/shard_map/ppermute | solution.py:19
  5.8 0.1 shard_map.83.own_edges
  5.9 0.0 copy-done.2
  5.9 0.0 copy-done.3
  5.9 0.0 copy-start
  6.0 0.0 copy-start.1
  6.0 2.1 %collective-permute-start.1 = (f32[104,256]{1,0:T(8,128)S(1)}, f32[104,256]{1,0:T(8,128)S(1)}, u32[]{:S(2)}, u32[]{:S(2)}) collective-permute-start(f32[104,256]{1,0:T(8,128)S(1)} %shard_map.85), channel_id=1, source_target_pairs={{0,1},{1,2},{2,3},{3,4},{4,5},{5,6},{6,7},{7,8},{8,9},{9,10},{10,1... | collective-permute-start | bytes 319496 | tf_op jit(solution)/shard_map/ppermute | solution.py:19
  8.0 0.0 copy-done
  8.0 0.7 %shard_map.82 = (bf16[64,1024]{1,0:T(8,128)(2,1)S(1)}, bf16[64,1024]{1,0:T(8,128)(2,1)S(1)}, bf16[1024,1024]{1,0:T(8,128)(2,1)S(1)}) custom-call(bf16[72,1024]{1,0:T(8,128)(2,1)S(1)} %fusion.1.message, bf16[1024,1024]{1,0:T(8,128)(2,1)S(1)} %copy-done), custom_call_target="tpu_custom_call" | custom-call | flops 10000000000 | bytes 4194304 | tf_op jit(solution)/shard_map/pallas_call | solution.py:145
  8.8 2.1 %collective-permute-done.message = bf16[72,1024]{1,0:T(8,128)(2,1)S(1)} collective-permute-done((bf16[72,1024]{1,0:T(8,128)(2,1)S(1)}, bf16[72,1024]{1,0:T(8,128)(2,1)S(1)}, u32[]{:S(2)}, u32[]{:S(2)}) %collective-permute-start) | collective-permute-done | bytes 147488 | tf_op jit(solution)/shard_map/ppermute | solution.py:19
  10.9 0.0 copy-done.1
  10.9 1.5 %shard_map.84 = (bf16[8,400,128]{2,1,0:T(8,128)(2,1)S(1)}, f32[100,512]{1,0:T(8,128)S(1)}, f32[1024,512]{1,0:T(8,128)S(1)}, bf16[128,512]{1,0:T(8,128)(2,1)S(1)}) custom-call(bf16[72,1024]{1,0:T(8,128)(2,1)S(1)} %collective-permute-done.message, bf16[64,1024]{1,0:T(8,128)(2,1)S(1)} %get-tuple-element.19.own_top, ...), custom_call_target="tpu_custom_call" | custom-call | flops 10000000000 | bytes 4194304 | tf_op jit(solution)/shard_map/pallas_call | solution.py:145
  12.4 0.6 %collective-permute-done.1.moved = f32[104,256]{1,0:T(8,128)S(1)} collective-permute-done((f32[104,256]{1,0:T(8,128)S(1)}, f32[104,256]{1,0:T(8,128)S(1)}, u32[]{:S(2)}, u32[]{:S(2)}) %collective-permute-start.1) | collective-permute-done | bytes 106528 | tf_op jit(solution)/shard_map/ppermute | solution.py:19
  13.0 14.3 %all_to_all.5.every = bf16[8,400,128]{2,1,0:T(8,128)(2,1)S(1)} all-to-all(bf16[8,400,128]{2,1,0:T(8,128)(2,1)S(1)} %get-tuple-element.25), channel_id=1, replica_groups=mesh['member'=8,'space'=64] {'member'}, dimensions={0} | all-to-all | bytes 1638400 | tf_op jit(solution)/shard_map/all_to_all | solution.py:208
  27.3 1.7 %shard_map.86 = (f32[64,1024]{1,0:T(8,128)S(1)}, bf16[64,1024]{1,0:T(8,128)(2,1)S(1)}) custom-call(bf16[8,400,128]{2,1,0:T(8,128)(2,1)S(1)} %all_to_all.5.every, f32[104,256]{1,0:T(8,128)S(1)} %collective-permute-done.1.moved, f32[100,512]{1,0:T(8,128)S(1)} %copy-done.2, f32[1,512]{1,0:T(1,128)S(1)} %bitcast.5, bf16[100,1024]{1,0:T(8,128)(2,1)S(1)} %copy-done.1, ...), custom_call_target="tpu_custom_call" | custom-call | flops 10000000000 | bytes 4194304 | tf_op jit(solution)/shard_map/pallas_call | solution.py:145
  29.0 12.2 %collective-permute-start.2 = (bf16[64,1024]{1,0:T(8,128)(2,1)S(1)}, bf16[64,1024]{1,0:T(8,128)(2,1)S(1)}, u32[]{:S(2)}, u32[]{:S(2)}) collective-permute-start(bf16[64,1024]{1,0:T(8,128)(2,1)S(1)} %get-tuple-element.32), channel_id=1, source_target_pairs={{0,63},{1,0},{2,1},{3,2},{4,3},{5,4},{6,5},{7,6},{8,7},{9,8},{10,9... | collective-permute-start | bytes 393224 | tf_op jit(solution)/shard_map/ppermute | solution.py:19
  41.1 1.0 %collective-permute-done.2 = bf16[64,1024]{1,0:T(8,128)(2,1)S(1)} collective-permute-done((bf16[64,1024]{1,0:T(8,128)(2,1)S(1)}, bf16[64,1024]{1,0:T(8,128)(2,1)S(1)}, u32[]{:S(2)}, u32[]{:S(2)}) %collective-permute-start.2) | collective-permute-done | bytes 131104 | tf_op jit(solution)/shard_map/ppermute | solution.py:19
  42.1 0.7 %fusion.2 = bf16[1,64,1024]{2,1,0:T(8,128)(2,1)} fusion(f32[64,1024]{1,0:T(8,128)S(1)} %get-tuple-element.31, bf16[64,1024]{1,0:T(8,128)(2,1)S(1)} %collective-permute-done.2), kind=kLoop, calls=%fused_computation.5 | loop fusion | flops 196608 | bytes 524288 | tf_op jit(solution)/shard_map/broadcast_in_dim | solution.py:217
  (3 shorter events, 0.0 us)
Async XLA Ops:
  1.1 4.8 %copy-start.2 = (f32[100,512]{1,0:T(8,128)S(1)}, f32[100,512]{1,0:T(8,128)}, u32[]{:S(2)}) copy-start(f32[100,512]{1,0:T(8,128)} %targets.1) | copy-start | bytes 614404
  1.1 4.8 %copy-start.3 = (f32[512]{0:T(512)S(1)}, f32[512]{0:T(512)}, u32[]{:S(2)}) copy-start(f32[512]{0:T(512)} %param.12) | copy-start | bytes 6148
  1.1 9.8 %collective-permute-start = (bf16[72,1024]{1,0:T(8,128)(2,1)S(1)}, bf16[72,1024]{1,0:T(8,128)(2,1)S(1)}, u32[]{:S(2)}, u32[]{:S(2)}) collective-permute-start(bf16[72,1024]{1,0:T(8,128)(2,1)S(1)} %fusion.1.message), channel_id=1, source_target_pairs={{0,1},{1,2},{2,3},{3,4},{4,5},{5,6},{6,7},{7,8},{8,9},{9,10},{10,1... | collective-permute-start | bytes 442376 | tf_op jit(solution)/shard_map/ppermute | solution.py:19
  5.9 2.1 %copy-start = (bf16[1024,1024]{1,0:T(8,128)(2,1)S(1)}, bf16[1024,1024]{1,0:T(8,128)(2,1)}, u32[]{:S(2)}) copy-start(bf16[1024,1024]{1,0:T(8,128)(2,1)} %w_in.3) | copy-start | bytes 6291460
  6.0 4.9 %copy-start.1 = (bf16[100,1024]{1,0:T(8,128)(2,1)S(1)}, bf16[100,1024]{1,0:T(8,128)(2,1)}, u32[]{:S(2)}) copy-start(bf16[100,1024]{1,0:T(8,128)(2,1)} %w_out.3) | copy-start | bytes 614404
  6.0 7.0 %collective-permute-start.1 = (f32[104,256]{1,0:T(8,128)S(1)}, f32[104,256]{1,0:T(8,128)S(1)}, u32[]{:S(2)}, u32[]{:S(2)}) collective-permute-start(f32[104,256]{1,0:T(8,128)S(1)} %shard_map.85), channel_id=1, source_target_pairs={{0,1},{1,2},{2,3},{3,4},{4,5},{5,6},{6,7},{7,8},{8,9},{9,10},{10,1... | collective-permute-start | bytes 319496 | tf_op jit(solution)/shard_map/ppermute | solution.py:19
  29.0 13.1 %collective-permute-start.2 = (bf16[64,1024]{1,0:T(8,128)(2,1)S(1)}, bf16[64,1024]{1,0:T(8,128)(2,1)S(1)}, u32[]{:S(2)}, u32[]{:S(2)}) collective-permute-start(bf16[64,1024]{1,0:T(8,128)(2,1)S(1)} %get-tuple-element.32), channel_id=1, source_target_pairs={{0,63},{1,0},{2,1},{3,2},{4,3},{5,4},{6,5},{7,6},{8,7},{9,8},{10,9... | collective-permute-start | bytes 393224 | tf_op jit(solution)/shard_map/ppermute | solution.py:19

commit v7 on v6

--- a/solution.py
+++ b/solution.py
@@ -162,7 +162,7 @@
     members = lax.axis_size("member")
     span = 2 * rows
 
-    tall = rows + 8
+    tall = rows + 16
     row = lax.broadcasted_iota(jnp.int32, (tall, channels), 0)
     column = lax.broadcasted_iota(jnp.int32, (tall, channels), 1)
 

time: 43 us -> 43.1 us (level)
  no operation moved by 1% of the time
where the time goes in v7:
time: 43.1 us; the launch traced here: 42.8 us
  starting transfers between devices  19 us (44%)
  blocking collectives  14.3 us (33%)
  Pallas kernels  3.95 us (9%)
  waiting for transfers between devices  3.7 us (9%)
  other arithmetic  1.77 us (4%)
    ppermute x3, starting transfers between devices, shifted(): lax.ppermute(block, axis, [(i, (i + by) % size) for i in range(size)])  19 us
    all_to_all x1, blocking collectives, per_device(): every = lax.all_to_all(copies, 'member', 0, 0, tiled=True)  14.3 us
    pallas_call x5, Pallas kernels, call(): pl.pallas_call(kernel, out_shape=[jax.ShapeDtypeStruct(dims, kind) for _,...  3.95 us
    ppermute x3, waiting for transfers between devices, shifted(): lax.ppermute(block, axis, [(i, (i + by) % size) for i in range(size)])  3.7 us
    select_n x1, other arithmetic, per_device(): message = jnp.where(row < rows, placed(latent[0], 0), edge)  1.07 us
  transfers between devices with their start and end apart: 3, of which 3 were waited for; matrix products, arithmetic and copies ran while one was open for 0% of the time, Pallas kernels for 5%

profile of v7, /device:TPU:1, one launch (start us, length us, event | category | flops | bytes accessed | tf_op | source)
XLA Modules:
  0.0 42.8 jit_solution(169232887627518434)
XLA Ops:
  0.0 1.1 %fusion.1.message = bf16[80,1024]{1,0:T(8,128)(2,1)S(1)} fusion(s32[4,512]{1,0:T(4,128)} %param.9, s32[4,512]{1,0:T(4,128)} %param.10, bf16[4,512]{1,0:T(4,128)(2,1)} %param.11, s32[1024]{0:T(1024)S(1)} %subtract_multiply_fusion, bf16[64,1024]{1,0:T(8,128)(2,1)} %bitcast.6, pred[80]{0:T(512)(128)(4,1)S(1)} %get-tuple-element.33, ...), kind=kLoop, calls=%fused_computation.4 | loop fusion | flops 737280 | bytes 319648 | tf_op jit(solution)/shard_map/jit(_where)/select_n | solution.py:176
  1.1 0.0 copy-start.2
  1.1 0.0 copy-start.3
  1.1 4.7 %collective-permute-start = (bf16[80,1024]{1,0:T(8,128)(2,1)S(1)}, bf16[80,1024]{1,0:T(8,128)(2,1)S(1)}, u32[]{:S(2)}, u32[]{:S(2)}) collective-permute-start(bf16[80,1024]{1,0:T(8,128)(2,1)S(1)} %fusion.1.message), channel_id=1, source_target_pairs={{0,1},{1,2},{2,3},{3,4},{4,5},{5,6},{6,7},{7,8},{8,9},{9,10},{10,1... | collective-permute-start | bytes 491528 | tf_op jit(solution)/shard_map/ppermute | solution.py:19
  5.8 0.1 shard_map.83.own_edges
  5.9 0.0 copy-done.2
  5.9 0.0 copy-done.3
  5.9 0.0 copy-start
  6.0 0.0 copy-start.1
  6.0 2.1 %collective-permute-start.1 = (f32[104,256]{1,0:T(8,128)S(1)}, f32[104,256]{1,0:T(8,128)S(1)}, u32[]{:S(2)}, u32[]{:S(2)}) collective-permute-start(f32[104,256]{1,0:T(8,128)S(1)} %shard_map.85), channel_id=1, source_target_pairs={{0,1},{1,2},{2,3},{3,4},{4,5},{5,6},{6,7},{7,8},{8,9},{9,10},{10,1... | collective-permute-start | bytes 319496 | tf_op jit(solution)/shard_map/ppermute | solution.py:19
  8.0 0.0 copy-done
  8.0 0.7 %shard_map.82 = (bf16[64,1024]{1,0:T(8,128)(2,1)S(1)}, bf16[64,1024]{1,0:T(8,128)(2,1)S(1)}, bf16[1024,1024]{1,0:T(8,128)(2,1)S(1)}) custom-call(bf16[80,1024]{1,0:T(8,128)(2,1)S(1)} %fusion.1.message, bf16[1024,1024]{1,0:T(8,128)(2,1)S(1)} %copy-done), custom_call_target="tpu_custom_call" | custom-call | flops 10000000000 | bytes 4194304 | tf_op jit(solution)/shard_map/pallas_call | solution.py:145
  8.8 2.1 %collective-permute-done.message = bf16[80,1024]{1,0:T(8,128)(2,1)S(1)} collective-permute-done((bf16[80,1024]{1,0:T(8,128)(2,1)S(1)}, bf16[80,1024]{1,0:T(8,128)(2,1)S(1)}, u32[]{:S(2)}, u32[]{:S(2)}) %collective-permute-start) | collective-permute-done | bytes 163872 | tf_op jit(solution)/shard_map/ppermute | solution.py:19
  10.9 0.0 copy-done.1
  10.9 1.5 %shard_map.84 = (bf16[8,400,128]{2,1,0:T(8,128)(2,1)S(1)}, f32[100,512]{1,0:T(8,128)S(1)}, f32[1024,512]{1,0:T(8,128)S(1)}, bf16[128,512]{1,0:T(8,128)(2,1)S(1)}) custom-call(bf16[80,1024]{1,0:T(8,128)(2,1)S(1)} %collective-permute-done.message, bf16[64,1024]{1,0:T(8,128)(2,1)S(1)} %get-tuple-element.19.own_top, ...), custom_call_target="tpu_custom_call" | custom-call | flops 10000000000 | bytes 4194304 | tf_op jit(solution)/shard_map/pallas_call | solution.py:145
  12.4 0.6 %collective-permute-done.1.moved = f32[104,256]{1,0:T(8,128)S(1)} collective-permute-done((f32[104,256]{1,0:T(8,128)S(1)}, f32[104,256]{1,0:T(8,128)S(1)}, u32[]{:S(2)}, u32[]{:S(2)}) %collective-permute-start.1) | collective-permute-done | bytes 106528 | tf_op jit(solution)/shard_map/ppermute | solution.py:19
  13.0 14.3 %all_to_all.5.every = bf16[8,400,128]{2,1,0:T(8,128)(2,1)S(1)} all-to-all(bf16[8,400,128]{2,1,0:T(8,128)(2,1)S(1)} %get-tuple-element.25), channel_id=1, replica_groups=mesh['member'=8,'space'=64] {'member'}, dimensions={0} | all-to-all | bytes 1638400 | tf_op jit(solution)/shard_map/all_to_all | solution.py:208
  27.3 1.7 %shard_map.86 = (f32[64,1024]{1,0:T(8,128)S(1)}, bf16[64,1024]{1,0:T(8,128)(2,1)S(1)}) custom-call(bf16[8,400,128]{2,1,0:T(8,128)(2,1)S(1)} %all_to_all.5.every, f32[104,256]{1,0:T(8,128)S(1)} %collective-permute-done.1.moved, f32[100,512]{1,0:T(8,128)S(1)} %copy-done.2, f32[1,512]{1,0:T(1,128)S(1)} %bitcast.5, bf16[100,1024]{1,0:T(8,128)(2,1)S(1)} %copy-done.1, ...), custom_call_target="tpu_custom_call" | custom-call | flops 10000000000 | bytes 4194304 | tf_op jit(solution)/shard_map/pallas_call | solution.py:145
  29.0 12.2 %collective-permute-start.2 = (bf16[64,1024]{1,0:T(8,128)(2,1)S(1)}, bf16[64,1024]{1,0:T(8,128)(2,1)S(1)}, u32[]{:S(2)}, u32[]{:S(2)}) collective-permute-start(bf16[64,1024]{1,0:T(8,128)(2,1)S(1)} %get-tuple-element.32), channel_id=1, source_target_pairs={{0,63},{1,0},{2,1},{3,2},{4,3},{5,4},{6,5},{7,6},{8,7},{9,8},{10,9... | collective-permute-start | bytes 393224 | tf_op jit(solution)/shard_map/ppermute | solution.py:19
  41.2 1.0 %collective-permute-done.2 = bf16[64,1024]{1,0:T(8,128)(2,1)S(1)} collective-permute-done((bf16[64,1024]{1,0:T(8,128)(2,1)S(1)}, bf16[64,1024]{1,0:T(8,128)(2,1)S(1)}, u32[]{:S(2)}, u32[]{:S(2)}) %collective-permute-start.2) | collective-permute-done | bytes 131104 | tf_op jit(solution)/shard_map/ppermute | solution.py:19
  42.1 0.7 %fusion.2 = bf16[1,64,1024]{2,1,0:T(8,128)(2,1)} fusion(f32[64,1024]{1,0:T(8,128)S(1)} %get-tuple-element.31, bf16[64,1024]{1,0:T(8,128)(2,1)S(1)} %collective-permute-done.2), kind=kLoop, calls=%fused_computation.5 | loop fusion | flops 196608 | bytes 524288 | tf_op jit(solution)/shard_map/broadcast_in_dim | solution.py:217
  (3 shorter events, 0.0 us)
Async XLA Ops:
  1.1 4.8 %copy-start.2 = (f32[100,512]{1,0:T(8,128)S(1)}, f32[100,512]{1,0:T(8,128)}, u32[]{:S(2)}) copy-start(f32[100,512]{1,0:T(8,128)} %targets.1) | copy-start | bytes 614404
  1.1 4.8 %copy-start.3 = (f32[512]{0:T(512)S(1)}, f32[512]{0:T(512)}, u32[]{:S(2)}) copy-start(f32[512]{0:T(512)} %param.12) | copy-start | bytes 6148
  1.1 9.8 %collective-permute-start = (bf16[80,1024]{1,0:T(8,128)(2,1)S(1)}, bf16[80,1024]{1,0:T(8,128)(2,1)S(1)}, u32[]{:S(2)}, u32[]{:S(2)}) collective-permute-start(bf16[80,1024]{1,0:T(8,128)(2,1)S(1)} %fusion.1.message), channel_id=1, source_target_pairs={{0,1},{1,2},{2,3},{3,4},{4,5},{5,6},{6,7},{7,8},{8,9},{9,10},{10,1... | collective-permute-start | bytes 491528 | tf_op jit(solution)/shard_map/ppermute | solution.py:19
  5.9 2.1 %copy-start = (bf16[1024,1024]{1,0:T(8,128)(2,1)S(1)}, bf16[1024,1024]{1,0:T(8,128)(2,1)}, u32[]{:S(2)}) copy-start(bf16[1024,1024]{1,0:T(8,128)(2,1)} %w_in.3) | copy-start | bytes 6291460
  6.0 5.0 %copy-start.1 = (bf16[100,1024]{1,0:T(8,128)(2,1)S(1)}, bf16[100,1024]{1,0:T(8,128)(2,1)}, u32[]{:S(2)}) copy-start(bf16[100,1024]{1,0:T(8,128)(2,1)} %w_out.3) | copy-start | bytes 614404
  6.0 7.0 %collective-permute-start.1 = (f32[104,256]{1,0:T(8,128)S(1)}, f32[104,256]{1,0:T(8,128)S(1)}, u32[]{:S(2)}, u32[]{:S(2)}) collective-permute-start(f32[104,256]{1,0:T(8,128)S(1)} %shard_map.85), channel_id=1, source_target_pairs={{0,1},{1,2},{2,3},{3,4},{4,5},{5,6},{6,7},{7,8},{8,9},{9,10},{10,1... | collective-permute-start | bytes 319496 | tf_op jit(solution)/shard_map/ppermute | solution.py:19
  29.0 13.2 %collective-permute-start.2 = (bf16[64,1024]{1,0:T(8,128)(2,1)S(1)}, bf16[64,1024]{1,0:T(8,128)(2,1)S(1)}, u32[]{:S(2)}, u32[]{:S(2)}) collective-permute-start(bf16[64,1024]{1,0:T(8,128)(2,1)S(1)} %get-tuple-element.32), channel_id=1, source_target_pairs={{0,63},{1,0},{2,1},{3,2},{4,3},{5,4},{6,5},{7,6},{8,7},{9,8},{10,9... | collective-permute-start | bytes 393224 | tf_op jit(solution)/shard_map/ppermute | solution.py:19

commit v8 on v7

--- a/solution.py
+++ b/solution.py
@@ -37,11 +37,6 @@
     return total.astype(bf16)
 
 
-def halves(part):
-    top = part.astype(bf16)
-    return top, (part - top.astype(f32)).astype(bf16)
-
-
 def goal_kernel(targets, area, message):
     count, half = targets.shape[0], message.shape[1]
     message[:count] = targets[:, half:]
@@ -69,35 +64,30 @@
     own_edges[...] = adjacent(span, message[span // 2 :, :half].astype(f32))
 
 
-def own_kernel(message, w_in, own_top, own_rest, turned):
-    rows, channels = own_top.shape
-    for c in range(0, channels, STEP):
-        cut = slice(c, c + STEP)
-        part = product(message[:rows], w_in[:, cut], ((1,), (0,)))
-        own_top[:, cut], own_rest[:, cut] = halves(part)
+def own_kernel(message, w_in, own_mixed, turned):
+    rows, channels = own_mixed.shape
+    for c in range(0, channels, STEP):
+        cut = slice(c, c + STEP)
+        own_mixed[:, cut] = product(message[:rows], w_in[:, cut], ((1,), (0,))).astype(bf16)
     for c in range(0, channels, STEP):
         cut = slice(c, c + STEP)
         turned[:, cut] = w_in[cut].T
 
 
 def forward_kernel(
-    message, own_top, own_rest, own_edges, w_in, w_out, copies, field, gate, edges, mixed, hidden
+    message, own_mixed, own_edges, w_in, w_out, copies, field, gate, edges, mixed, hidden
 ):
-    rows, channels = own_top.shape
+    rows, channels = own_mixed.shape
     span, half = own_edges.shape
     edges[:, :half] = adjacent(span, message[rows:, half : 2 * half].astype(f32))
     edges[:, half:] = own_edges[...]
-    both = edges[...]
-    twice = jnp.concatenate([both, both], axis=0)
-    for c in range(0, channels, STEP):
-        cut = slice(c, c + STEP)
-        part = product(message[:rows], w_in[:, cut], ((1,), (0,)))
-        mixed[:rows, cut], mixed[span : span + rows, cut] = halves(part)
-    mixed[rows:span] = own_top[...]
-    mixed[span + rows :] = own_rest[...]
-    for c in range(0, channels, STEP):
-        cut = slice(c, c + STEP)
-        pre = product(mixed[:, cut], twice, ((0,), (0,)))
+    for c in range(0, channels, STEP):
+        cut = slice(c, c + STEP)
+        mixed[:rows, cut] = product(message[:rows], w_in[:, cut], ((1,), (0,))).astype(bf16)
+    mixed[rows:] = own_mixed[...]
+    for c in range(0, channels, STEP):
+        cut = slice(c, c + STEP)
+        pre = product(mixed[:, cut], edges[...], ((0,), (0,)))
         sigma = 1.0 / (1.0 + jnp.exp(-pre))
         act = pre * sigma
         hidden[cut] = act.astype(bf16)
@@ -119,8 +109,8 @@
     me = lax.axis_index("member")
     own = every[me].astype(f32)
     total = jnp.zeros(own.shape, f32)
-    for m in range(members):
-        total = total + slope(own - every[m].astype(f32))
+    for step in range(1, members):
+        total = total + slope(own - every[lax.rem(me + step, members)].astype(f32))
     total = unpacked(total, count)
     goal = jnp.concatenate([moved[:count], targets[:, :half]], axis=1)
     scale = jnp.concatenate([moved[count : count + 1], area[:, :half]], axis=1)
@@ -181,28 +171,24 @@
         goal_kernel, LIMITS[0], [(HERE, targets), (HERE, area)], [(HERE, (fields + 4, half), f32)], []
     )
     moved = shifted(goals, "space", 1)
-    own_top, own_rest, turned = call(
+    own_mixed, turned = call(
         own_kernel,
         LIMITS[0],
         [(HERE, message), (HERE, w_in)],
-        [
-            (HERE, (rows, channels), bf16),
-            (HERE, (rows, channels), bf16),
-            (HERE, (channels, channels), bf16),
-        ],
+        [(HERE, (rows, channels), bf16), (HERE, (channels, channels), bf16)],
         [],
     )
     copies, field, gate, edges = call(
         forward_kernel,
         LIMITS[1],
-        [(HERE, x) for x in (received, own_top, own_rest, own_edges, w_in, w_out)],
+        [(HERE, x) for x in (received, own_mixed, own_edges, w_in, w_out)],
         [
             (HERE, (members, fields * points // LANES, LANES), bf16),
             (HERE, (fields, points), f32),
             (HERE, (channels, points), f32),
             (HERE, (span, points), bf16),
         ],
-        [((2 * span, channels), bf16), ((channels, points), bf16)],
+        [((span, channels), bf16), ((channels, points), bf16)],
     )
     copies, moved = lax.optimization_barrier((copies, moved))
     every = lax.all_to_all(copies, "member", 0, 0, tiled=True)

time: 43.1 us -> 43 us (level)
  no operation moved by 1% of the time
where the time goes in v8:
time: 43 us; the launch traced here: 42.8 us
  starting transfers between devices  19 us (44%)
  blocking collectives  14.2 us (33%)
  Pallas kernels  3.87 us (9%)
  waiting for transfers between devices  3.74 us (9%)
  other arithmetic  1.77 us (4%)
    ppermute x3, starting transfers between devices, shifted(): lax.ppermute(block, axis, [(i, (i + by) % size) for i in range(size)])  19 us
    all_to_all x1, blocking collectives, per_device(): every = lax.all_to_all(copies, 'member', 0, 0, tiled=True)  14.2 us
    pallas_call x5, Pallas kernels, call(): pl.pallas_call(kernel, out_shape=[jax.ShapeDtypeStruct(dims, kind) for _,...  3.87 us
    ppermute x3, waiting for transfers between devices, shifted(): lax.ppermute(block, axis, [(i, (i + by) % size) for i in range(size)])  3.74 us
    select_n x1, other arithmetic, per_device(): message = jnp.where(row < rows, placed(latent[0], 0), edge)  1.07 us
  transfers between devices with their start and end apart: 3, of which 3 were waited for; matrix products, arithmetic and copies ran while one was open for 0% of the time, Pallas kernels for 5%

profile of v8, /device:TPU:1, one launch (start us, length us, event | category | flops | bytes accessed | tf_op | source)
XLA Modules:
  0.0 42.8 jit_solution(11939920327828897273)
XLA Ops:
  0.0 1.1 %fusion.1.message = bf16[80,1024]{1,0:T(8,128)(2,1)S(1)} fusion(s32[4,512]{1,0:T(4,128)} %param.9, s32[4,512]{1,0:T(4,128)} %param.10, bf16[4,512]{1,0:T(4,128)(2,1)} %param.11, s32[1024]{0:T(1024)S(1)} %subtract_multiply_fusion, bf16[64,1024]{1,0:T(8,128)(2,1)} %bitcast.6, pred[80]{0:T(512)(128)(4,1)S(1)} %get-tuple-element.31, ...), kind=kLoop, calls=%fused_computation.4 | loop fusion | flops 737280 | bytes 319648 | tf_op jit(solution)/shard_map/jit(_where)/select_n | solution.py:166
  1.1 0.0 copy-start.2
  1.1 0.0 copy-start.3
  1.1 4.7 %collective-permute-start = (bf16[80,1024]{1,0:T(8,128)(2,1)S(1)}, bf16[80,1024]{1,0:T(8,128)(2,1)S(1)}, u32[]{:S(2)}, u32[]{:S(2)}) collective-permute-start(bf16[80,1024]{1,0:T(8,128)(2,1)S(1)} %fusion.1.message), channel_id=1, source_target_pairs={{0,1},{1,2},{2,3},{3,4},{4,5},{5,6},{6,7},{7,8},{8,9},{9,10},{10,1... | collective-permute-start | bytes 491528 | tf_op jit(solution)/shard_map/ppermute | solution.py:19
  5.8 0.1 shard_map.83.own_edges
  5.9 0.0 copy-done.2
  5.9 0.0 copy-done.3
  5.9 0.0 copy-start
  6.0 0.0 copy-start.1
  6.0 2.1 %collective-permute-start.1 = (f32[104,256]{1,0:T(8,128)S(1)}, f32[104,256]{1,0:T(8,128)S(1)}, u32[]{:S(2)}, u32[]{:S(2)}) collective-permute-start(f32[104,256]{1,0:T(8,128)S(1)} %shard_map.85), channel_id=1, source_target_pairs={{0,1},{1,2},{2,3},{3,4},{4,5},{5,6},{6,7},{7,8},{8,9},{9,10},{10,1... | collective-permute-start | bytes 319496 | tf_op jit(solution)/shard_map/ppermute | solution.py:19
  8.0 0.0 copy-done
  8.0 0.7 %shard_map.82 = (bf16[64,1024]{1,0:T(8,128)(2,1)S(1)}, bf16[1024,1024]{1,0:T(8,128)(2,1)S(1)}) custom-call(bf16[80,1024]{1,0:T(8,128)(2,1)S(1)} %fusion.1.message, bf16[1024,1024]{1,0:T(8,128)(2,1)S(1)} %copy-done), custom_call_target="tpu_custom_call" | custom-call | flops 10000000000 | bytes 4194304 | tf_op jit(solution)/shard_map/pallas_call | solution.py:135
  8.7 2.2 %collective-permute-done.message = bf16[80,1024]{1,0:T(8,128)(2,1)S(1)} collective-permute-done((bf16[80,1024]{1,0:T(8,128)(2,1)S(1)}, bf16[80,1024]{1,0:T(8,128)(2,1)S(1)}, u32[]{:S(2)}, u32[]{:S(2)}) %collective-permute-start) | collective-permute-done | bytes 163872 | tf_op jit(solution)/shard_map/ppermute | solution.py:19
  10.9 0.0 copy-done.1
  10.9 1.5 %shard_map.84 = (bf16[8,400,128]{2,1,0:T(8,128)(2,1)S(1)}, f32[100,512]{1,0:T(8,128)S(1)}, f32[1024,512]{1,0:T(8,128)S(1)}, bf16[128,512]{1,0:T(8,128)(2,1)S(1)}) custom-call(bf16[80,1024]{1,0:T(8,128)(2,1)S(1)} %collective-permute-done.message, bf16[64,1024]{1,0:T(8,128)(2,1)S(1)} %get-tuple-element.18.own_mixed, bf16[128,256]{1,0:T(8,128)(2,1)S(1)} %shard_map.83.own_edges, ...), custom_call_target="tpu_custom_call" | custom-call | flops 10000000000 | bytes 4194304 | tf_op jit(solution)/shard_map/pallas_call | solution.py:135
  12.4 0.6 %collective-permute-done.1.moved = f32[104,256]{1,0:T(8,128)S(1)} collective-permute-done((f32[104,256]{1,0:T(8,128)S(1)}, f32[104,256]{1,0:T(8,128)S(1)}, u32[]{:S(2)}, u32[]{:S(2)}) %collective-permute-start.1) | collective-permute-done | bytes 106528 | tf_op jit(solution)/shard_map/ppermute | solution.py:19
  13.0 14.2 %all_to_all.5.every = bf16[8,400,128]{2,1,0:T(8,128)(2,1)S(1)} all-to-all(bf16[8,400,128]{2,1,0:T(8,128)(2,1)S(1)} %get-tuple-element.23), channel_id=1, replica_groups=mesh['member'=8,'space'=64] {'member'}, dimensions={0} | all-to-all | bytes 1638400 | tf_op jit(solution)/shard_map/all_to_all | solution.py:194
  27.3 1.6 %shard_map.86 = (f32[64,1024]{1,0:T(8,128)S(1)}, bf16[64,1024]{1,0:T(8,128)(2,1)S(1)}) custom-call(bf16[8,400,128]{2,1,0:T(8,128)(2,1)S(1)} %all_to_all.5.every, f32[104,256]{1,0:T(8,128)S(1)} %collective-permute-done.1.moved, f32[100,512]{1,0:T(8,128)S(1)} %copy-done.2, f32[1,512]{1,0:T(1,128)S(1)} %bitcast.5, bf16[100,1024]{1,0:T(8,128)(2,1)S(1)} %copy-done.1, ...), custom_call_target="tpu_custom_call" | custom-call | flops 10000000000 | bytes 4194304 | tf_op jit(solution)/shard_map/pallas_call | solution.py:135
  28.9 12.2 %collective-permute-start.2 = (bf16[64,1024]{1,0:T(8,128)(2,1)S(1)}, bf16[64,1024]{1,0:T(8,128)(2,1)S(1)}, u32[]{:S(2)}, u32[]{:S(2)}) collective-permute-start(bf16[64,1024]{1,0:T(8,128)(2,1)S(1)} %get-tuple-element.30), channel_id=1, source_target_pairs={{0,63},{1,0},{2,1},{3,2},{4,3},{5,4},{6,5},{7,6},{8,7},{9,8},{10,9... | collective-permute-start | bytes 393224 | tf_op jit(solution)/shard_map/ppermute | solution.py:19
  41.1 1.0 %collective-permute-done.2 = bf16[64,1024]{1,0:T(8,128)(2,1)S(1)} collective-permute-done((bf16[64,1024]{1,0:T(8,128)(2,1)S(1)}, bf16[64,1024]{1,0:T(8,128)(2,1)S(1)}, u32[]{:S(2)}, u32[]{:S(2)}) %collective-permute-start.2) | collective-permute-done | bytes 131104 | tf_op jit(solution)/shard_map/ppermute | solution.py:19
  42.1 0.7 %fusion.2 = bf16[1,64,1024]{2,1,0:T(8,128)(2,1)} fusion(f32[64,1024]{1,0:T(8,128)S(1)} %get-tuple-element.29, bf16[64,1024]{1,0:T(8,128)(2,1)S(1)} %collective-permute-done.2), kind=kLoop, calls=%fused_computation.5 | loop fusion | flops 196608 | bytes 524288 | tf_op jit(solution)/shard_map/broadcast_in_dim | solution.py:203
  (3 shorter events, 0.0 us)
Async XLA Ops:
  1.1 4.8 %copy-start.2 = (f32[100,512]{1,0:T(8,128)S(1)}, f32[100,512]{1,0:T(8,128)}, u32[]{:S(2)}) copy-start(f32[100,512]{1,0:T(8,128)} %targets.1) | copy-start | bytes 614404
  1.1 4.8 %copy-start.3 = (f32[512]{0:T(512)S(1)}, f32[512]{0:T(512)}, u32[]{:S(2)}) copy-start(f32[512]{0:T(512)} %param.12) | copy-start | bytes 6148
  1.1 9.8 %collective-permute-start = (bf16[80,1024]{1,0:T(8,128)(2,1)S(1)}, bf16[80,1024]{1,0:T(8,128)(2,1)S(1)}, u32[]{:S(2)}, u32[]{:S(2)}) collective-permute-start(bf16[80,1024]{1,0:T(8,128)(2,1)S(1)} %fusion.1.message), channel_id=1, source_target_pairs={{0,1},{1,2},{2,3},{3,4},{4,5},{5,6},{6,7},{7,8},{8,9},{9,10},{10,1... | collective-permute-start | bytes 491528 | tf_op jit(solution)/shard_map/ppermute | solution.py:19
  5.9 2.1 %copy-start = (bf16[1024,1024]{1,0:T(8,128)(2,1)S(1)}, bf16[1024,1024]{1,0:T(8,128)(2,1)}, u32[]{:S(2)}) copy-start(bf16[1024,1024]{1,0:T(8,128)(2,1)} %w_in.3) | copy-start | bytes 6291460
  6.0 5.0 %copy-start.1 = (bf16[100,1024]{1,0:T(8,128)(2,1)S(1)}, bf16[100,1024]{1,0:T(8,128)(2,1)}, u32[]{:S(2)}) copy-start(bf16[100,1024]{1,0:T(8,128)(2,1)} %w_out.3) | copy-start | bytes 614404
  6.0 7.0 %collective-permute-start.1 = (f32[104,256]{1,0:T(8,128)S(1)}, f32[104,256]{1,0:T(8,128)S(1)}, u32[]{:S(2)}, u32[]{:S(2)}) collective-permute-start(f32[104,256]{1,0:T(8,128)S(1)} %shard_map.85), channel_id=1, source_target_pairs={{0,1},{1,2},{2,3},{3,4},{4,5},{5,6},{6,7},{7,8},{8,9},{9,10},{10,1... | collective-permute-start | bytes 319496 | tf_op jit(solution)/shard_map/ppermute | solution.py:19
  28.9 13.2 %collective-permute-start.2 = (bf16[64,1024]{1,0:T(8,128)(2,1)S(1)}, bf16[64,1024]{1,0:T(8,128)(2,1)S(1)}, u32[]{:S(2)}, u32[]{:S(2)}) collective-permute-start(bf16[64,1024]{1,0:T(8,128)(2,1)S(1)} %get-tuple-element.30), channel_id=1, source_target_pairs={{0,63},{1,0},{2,1},{3,2},{4,3},{5,4},{6,5},{7,6},{8,7},{9,8},{10,9... | collective-permute-start | bytes 393224 | tf_op jit(solution)/shard_map/ppermute | solution.py:19

commit v9 on v7

--- a/solution.py
+++ b/solution.py
@@ -17,6 +17,11 @@
 def shifted(block, axis, by):
     size = lax.axis_size(axis)
     return lax.ppermute(block, axis, [(i, (i + by) % size) for i in range(size)])
+
+
+def alternate(members):
+    half = members // 2
+    return [half * (i % 2) + i // 2 for i in range(members)]
 
 
 def slope(diff):
@@ -116,7 +121,9 @@
     count, points = field.shape
     half = points // 2
     rows, channels = out.shape
-    me = lax.axis_index("member")
+    half_row = members // 2
+    member = lax.axis_index("member")
+    me = 2 * lax.rem(member, half_row) + member // half_row
     own = every[me].astype(f32)
     total = jnp.zeros(own.shape, f32)
     for m in range(members):
@@ -205,7 +212,7 @@
         [((2 * span, channels), bf16), ((channels, points), bf16)],
     )
     copies, moved = lax.optimization_barrier((copies, moved))
-    every = lax.all_to_all(copies, "member", 0, 0, tiled=True)
+    every = lax.all_to_all(copies, "member", 0, 0, tiled=True, axis_index_groups=[alternate(members)])
     inner, rim = call(
         backward_kernel,
         LIMITS[2],

time: 43.1 us -> 43 us (level)
  no operation moved by 1% of the time
where the time goes in v9:
time: 43 us; the launch traced here: 42.8 us
  starting transfers between devices  19 us (44%)
  blocking collectives  14.2 us (33%)
  Pallas kernels  3.96 us (9%)
  waiting for transfers between devices  3.7 us (9%)
  other arithmetic  1.77 us (4%)
    ppermute x3, starting transfers between devices, shifted(): lax.ppermute(block, axis, [(i, (i + by) % size) for i in range(size)])  19 us
    all_to_all x1, blocking collectives, per_device(): lax.all_to_all(copies, 'member', 0, 0, tiled=True, axis_index_groups=[alt...  14.2 us
    pallas_call x5, Pallas kernels, call(): pl.pallas_call(kernel, out_shape=[jax.ShapeDtypeStruct(dims, kind) for _,...  3.96 us
    ppermute x3, waiting for transfers between devices, shifted(): lax.ppermute(block, axis, [(i, (i + by) % size) for i in range(size)])  3.7 us
    select_n x1, other arithmetic, per_device(): message = jnp.where(row < rows, placed(latent[0], 0), edge)  1.07 us
  transfers between devices with their start and end apart: 3, of which 3 were waited for; matrix products, arithmetic and copies ran while one was open for 0% of the time, Pallas kernels for 5%

profile of v9, /device:TPU:1, one launch (start us, length us, event | category | flops | bytes accessed | tf_op | source)
XLA Modules:
  0.0 42.8 jit_solution(3043033180559135032)
XLA Ops:
  0.0 1.1 %fusion.1.message = bf16[80,1024]{1,0:T(8,128)(2,1)S(1)} fusion(s32[4,512]{1,0:T(4,128)} %param.9, s32[4,512]{1,0:T(4,128)} %param.10, bf16[4,512]{1,0:T(4,128)(2,1)} %param.11, s32[1024]{0:T(1024)S(1)} %subtract_multiply_fusion, bf16[64,1024]{1,0:T(8,128)(2,1)} %bitcast.6, pred[80]{0:T(512)(128)(4,1)S(1)} %get-tuple-element.33, ...), kind=kLoop, calls=%fused_computation.4 | loop fusion | flops 737280 | bytes 319648 | tf_op jit(solution)/shard_map/jit(_where)/select_n | solution.py:183
  1.1 0.0 copy-start.2
  1.1 0.0 copy-start.3
  1.1 4.7 %collective-permute-start = (bf16[80,1024]{1,0:T(8,128)(2,1)S(1)}, bf16[80,1024]{1,0:T(8,128)(2,1)S(1)}, u32[]{:S(2)}, u32[]{:S(2)}) collective-permute-start(bf16[80,1024]{1,0:T(8,128)(2,1)S(1)} %fusion.1.message), channel_id=1, source_target_pairs={{0,1},{1,2},{2,3},{3,4},{4,5},{5,6},{6,7},{7,8},{8,9},{9,10},{10,1... | collective-permute-start | bytes 491528 | tf_op jit(solution)/shard_map/ppermute | solution.py:19
  5.8 0.1 shard_map.83.own_edges
  5.9 0.0 copy-done.2
  5.9 0.0 copy-done.3
  5.9 0.0 copy-start
  6.0 0.0 copy-start.1
  6.0 2.1 %collective-permute-start.1 = (f32[104,256]{1,0:T(8,128)S(1)}, f32[104,256]{1,0:T(8,128)S(1)}, u32[]{:S(2)}, u32[]{:S(2)}) collective-permute-start(f32[104,256]{1,0:T(8,128)S(1)} %shard_map.85), channel_id=1, source_target_pairs={{0,1},{1,2},{2,3},{3,4},{4,5},{5,6},{6,7},{7,8},{8,9},{9,10},{10,1... | collective-permute-start | bytes 319496 | tf_op jit(solution)/shard_map/ppermute | solution.py:19
  8.0 0.0 copy-done
  8.0 0.7 %shard_map.82 = (bf16[64,1024]{1,0:T(8,128)(2,1)S(1)}, bf16[64,1024]{1,0:T(8,128)(2,1)S(1)}, bf16[1024,1024]{1,0:T(8,128)(2,1)S(1)}) custom-call(bf16[80,1024]{1,0:T(8,128)(2,1)S(1)} %fusion.1.message, bf16[1024,1024]{1,0:T(8,128)(2,1)S(1)} %copy-done), custom_call_target="tpu_custom_call" | custom-call | flops 10000000000 | bytes 4194304 | tf_op jit(solution)/shard_map/pallas_call | solution.py:152
  8.8 2.1 %collective-permute-done.message = bf16[80,1024]{1,0:T(8,128)(2,1)S(1)} collective-permute-done((bf16[80,1024]{1,0:T(8,128)(2,1)S(1)}, bf16[80,1024]{1,0:T(8,128)(2,1)S(1)}, u32[]{:S(2)}, u32[]{:S(2)}) %collective-permute-start) | collective-permute-done | bytes 163872 | tf_op jit(solution)/shard_map/ppermute | solution.py:19
  10.9 0.0 copy-done.1
  10.9 1.5 %shard_map.84 = (bf16[8,400,128]{2,1,0:T(8,128)(2,1)S(1)}, f32[100,512]{1,0:T(8,128)S(1)}, f32[1024,512]{1,0:T(8,128)S(1)}, bf16[128,512]{1,0:T(8,128)(2,1)S(1)}) custom-call(bf16[80,1024]{1,0:T(8,128)(2,1)S(1)} %collective-permute-done.message, bf16[64,1024]{1,0:T(8,128)(2,1)S(1)} %get-tuple-element.19.own_top, ...), custom_call_target="tpu_custom_call" | custom-call | flops 10000000000 | bytes 4194304 | tf_op jit(solution)/shard_map/pallas_call | solution.py:152
  12.4 0.6 %collective-permute-done.1.moved = f32[104,256]{1,0:T(8,128)S(1)} collective-permute-done((f32[104,256]{1,0:T(8,128)S(1)}, f32[104,256]{1,0:T(8,128)S(1)}, u32[]{:S(2)}, u32[]{:S(2)}) %collective-permute-start.1) | collective-permute-done | bytes 106528 | tf_op jit(solution)/shard_map/ppermute | solution.py:19
  13.0 14.2 %all_to_all.5.every = bf16[8,400,128]{2,1,0:T(8,128)(2,1)S(1)} all-to-all(bf16[8,400,128]{2,1,0:T(8,128)(2,1)S(1)} %get-tuple-element.25), channel_id=1, replica_groups={{0,256,64,320,128,384,192,448},{1,257,65,321,129,385,193,449},{2,258,66..., dimensions={0} | all-to-all | bytes 1638400 | tf_op jit(solution)/shard_map/all_to_all | solution.py:215
  27.3 1.7 %shard_map.86 = (f32[64,1024]{1,0:T(8,128)S(1)}, bf16[64,1024]{1,0:T(8,128)(2,1)S(1)}) custom-call(bf16[8,400,128]{2,1,0:T(8,128)(2,1)S(1)} %all_to_all.5.every, f32[104,256]{1,0:T(8,128)S(1)} %collective-permute-done.1.moved, f32[100,512]{1,0:T(8,128)S(1)} %copy-done.2, f32[1,512]{1,0:T(1,128)S(1)} %bitcast.5, bf16[100,1024]{1,0:T(8,128)(2,1)S(1)} %copy-done.1, ...), custom_call_target="tpu_custom_call" | custom-call | flops 10000000000 | bytes 4194304 | tf_op jit(solution)/shard_map/pallas_call | solution.py:152
  28.9 12.2 %collective-permute-start.2 = (bf16[64,1024]{1,0:T(8,128)(2,1)S(1)}, bf16[64,1024]{1,0:T(8,128)(2,1)S(1)}, u32[]{:S(2)}, u32[]{:S(2)}) collective-permute-start(bf16[64,1024]{1,0:T(8,128)(2,1)S(1)} %get-tuple-element.32), channel_id=1, source_target_pairs={{0,63},{1,0},{2,1},{3,2},{4,3},{5,4},{6,5},{7,6},{8,7},{9,8},{10,9... | collective-permute-start | bytes 393224 | tf_op jit(solution)/shard_map/ppermute | solution.py:19
  41.1 1.0 %collective-permute-done.2 = bf16[64,1024]{1,0:T(8,128)(2,1)S(1)} collective-permute-done((bf16[64,1024]{1,0:T(8,128)(2,1)S(1)}, bf16[64,1024]{1,0:T(8,128)(2,1)S(1)}, u32[]{:S(2)}, u32[]{:S(2)}) %collective-permute-start.2) | collective-permute-done | bytes 131104 | tf_op jit(solution)/shard_map/ppermute | solution.py:19
  42.1 0.7 %fusion.2 = bf16[1,64,1024]{2,1,0:T(8,128)(2,1)} fusion(f32[64,1024]{1,0:T(8,128)S(1)} %get-tuple-element.31, bf16[64,1024]{1,0:T(8,128)(2,1)S(1)} %collective-permute-done.2), kind=kLoop, calls=%fused_computation.5 | loop fusion | flops 196608 | bytes 524288 | tf_op jit(solution)/shard_map/broadcast_in_dim | solution.py:224
  (3 shorter events, 0.0 us)
Async XLA Ops:
  1.1 4.8 %copy-start.2 = (f32[100,512]{1,0:T(8,128)S(1)}, f32[100,512]{1,0:T(8,128)}, u32[]{:S(2)}) copy-start(f32[100,512]{1,0:T(8,128)} %targets.1) | copy-start | bytes 614404
  1.1 4.8 %copy-start.3 = (f32[512]{0:T(512)S(1)}, f32[512]{0:T(512)}, u32[]{:S(2)}) copy-start(f32[512]{0:T(512)} %param.12) | copy-start | bytes 6148
  1.1 9.8 %collective-permute-start = (bf16[80,1024]{1,0:T(8,128)(2,1)S(1)}, bf16[80,1024]{1,0:T(8,128)(2,1)S(1)}, u32[]{:S(2)}, u32[]{:S(2)}) collective-permute-start(bf16[80,1024]{1,0:T(8,128)(2,1)S(1)} %fusion.1.message), channel_id=1, source_target_pairs={{0,1},{1,2},{2,3},{3,4},{4,5},{5,6},{6,7},{7,8},{8,9},{9,10},{10,1... | collective-permute-start | bytes 491528 | tf_op jit(solution)/shard_map/ppermute | solution.py:19
  5.9 2.1 %copy-start = (bf16[1024,1024]{1,0:T(8,128)(2,1)S(1)}, bf16[1024,1024]{1,0:T(8,128)(2,1)}, u32[]{:S(2)}) copy-start(bf16[1024,1024]{1,0:T(8,128)(2,1)} %w_in.3) | copy-start | bytes 6291460
  6.0 5.0 %copy-start.1 = (bf16[100,1024]{1,0:T(8,128)(2,1)S(1)}, bf16[100,1024]{1,0:T(8,128)(2,1)}, u32[]{:S(2)}) copy-start(bf16[100,1024]{1,0:T(8,128)(2,1)} %w_out.3) | copy-start | bytes 614404
  6.0 7.0 %collective-permute-start.1 = (f32[104,256]{1,0:T(8,128)S(1)}, f32[104,256]{1,0:T(8,128)S(1)}, u32[]{:S(2)}, u32[]{:S(2)}) collective-permute-start(f32[104,256]{1,0:T(8,128)S(1)} %shard_map.85), channel_id=1, source_target_pairs={{0,1},{1,2},{2,3},{3,4},{4,5},{5,6},{6,7},{7,8},{8,9},{9,10},{10,1... | collective-permute-start | bytes 319496 | tf_op jit(solution)/shard_map/ppermute | solution.py:19
  28.9 13.2 %collective-permute-start.2 = (bf16[64,1024]{1,0:T(8,128)(2,1)S(1)}, bf16[64,1024]{1,0:T(8,128)(2,1)S(1)}, u32[]{:S(2)}, u32[]{:S(2)}) collective-permute-start(bf16[64,1024]{1,0:T(8,128)(2,1)S(1)} %get-tuple-element.32), channel_id=1, source_target_pairs={{0,63},{1,0},{2,1},{3,2},{4,3},{5,4},{6,5},{7,6},{8,7},{9,8},{10,9... | collective-permute-start | bytes 393224 | tf_op jit(solution)/shard_map/ppermute | solution.py:19
